TPU v7x, 128 devices: a whole 4x4x4 slice. The times are simulated.
128 devices in a mesh: frame: 128 (over z, x, y, core).
Axes of the slice: x: 4, y: 4, z: 4, core: 2. Of those that a mesh axis runs over, the one named last changes fastest.
Arguments:
- inputs: bfloat16 [24576, 3072], P('frame'), may hold values from -6 to 6
- queries: bfloat16 [24576, 1536], P('frame'), may hold values from -5 to 5
- keys: bfloat16 [24576, 1536], P('frame'), may hold values from -5 to 5
- values: bfloat16 [24576, 1536], P('frame'), may hold values from -6 to 6
- output_gradient: bfloat16 [24576, 1536], P('frame'), may hold values from -48 to 48
- radial_block_mask: int32 [128, 128], replicated, may hold values from 0 to 1, as said below
- adapter_down_weight: bfloat16 [3, 3072, 64], replicated, may hold values from -0.109375 to 0.109375
- adapter_up_weight: bfloat16 [3, 64, 1536], replicated, may hold values from -0.75 to 0.75
Outputs:
- grad_input: bfloat16 [24576, 3072], P('frame')
- down_gradient: float32 [3, 3072, 64], replicated
- up_gradient: float32 [3, 64, 1536], replicated
Inputs may be any that keep to these rules, and one draw needn't show every extreme that they name: radial_block_mask[b, c] is 1 whenever |b - c| <= 1, and 0 unless |b - c| is 0 or a power of two below 128.
All inputs are finite; a program needn't handle non-finite values.
Results may differ from a plain program's by a relative error of at most 0.0099.
Values may be sent and summed in bfloat16 or wider, within the bound.
A program may use at most 192 MiB of HBM per device.

v0:
```python
import math

import jax
import jax.numpy as jnp
from jax import lax
from jax.sharding import PartitionSpec as P

DH = 128


def passed_along(value, axis, steps):
    count = lax.axis_size(axis)
    initial, last = (max(0, -steps), min(count, count - steps))
    return lax.ppermute(value, axis, [(source, source + steps) for source in range(initial, last)])


def block_grads(q_block, g_block, key_blocks, val_blocks, keep_bits):
    block_count, row_count, feat_width = key_blocks.shape
    head_count = feat_width // DH
    inv_root = 1.0 / math.sqrt(DH)
    flat_keys = key_blocks.reshape(block_count * row_count, feat_width)
    flat_vals = val_blocks.reshape(block_count * row_count, feat_width)
    live_cols = jnp.repeat(keep_bits, row_count, total_repeat_length=block_count * row_count) > 0.5

    def per_head(head_id, running):
        q_acc, k_acc, v_acc = running
        col_start = (head_id * DH).astype(jnp.int32)
        q_head = lax.dynamic_slice_in_dim(q_block, col_start, DH, 1)
        g_head = lax.dynamic_slice_in_dim(g_block, col_start, DH, 1)
        k_head = lax.dynamic_slice_in_dim(flat_keys, col_start, DH, 1)
        v_head = lax.dynamic_slice_in_dim(flat_vals, col_start, DH, 1)
        scores = jnp.dot(q_head, k_head.T, preferred_element_type=jnp.float32) * inv_root
        scores = jnp.where(live_cols[None, :], scores, -1e30)
        row_max = jnp.max(scores, axis=1, keepdims=True)
        row_sum = jnp.sum(jnp.exp(scores - row_max), axis=1, keepdims=True)
        log_total = row_max + jnp.log(row_sum)
        probs = jnp.exp(scores - log_total)
        probs_b = probs.astype(jnp.bfloat16)
        attended = jnp.dot(probs_b, v_head, preferred_element_type=jnp.float32)
        row_dot = jnp.sum(g_head.astype(jnp.float32) * attended, axis=1, keepdims=True)
        dprobs = jnp.dot(g_head, v_head.T, preferred_element_type=jnp.float32)
        dscores = (probs * (dprobs - row_dot)).astype(jnp.bfloat16)
        q_grad = jnp.dot(dscores, k_head, preferred_element_type=jnp.float32) * inv_root
        k_grad = (jnp.dot(dscores.T, q_head, preferred_element_type=jnp.float32) * inv_root).astype(
            jnp.bfloat16
        )
        v_grad = jnp.dot(probs_b.T, g_head, preferred_element_type=jnp.float32).astype(jnp.bfloat16)
        q_acc = lax.dynamic_update_slice_in_dim(q_acc, q_grad, col_start, 1)
        k_acc = lax.dynamic_update_slice_in_dim(k_acc, k_grad, col_start, 1)
        v_acc = lax.dynamic_update_slice_in_dim(v_acc, v_grad, col_start, 1)
        return (q_acc, k_acc, v_acc)

    start_state = (
        jnp.zeros((row_count, feat_width), jnp.float32),
        jnp.zeros((block_count * row_count, feat_width), jnp.bfloat16),
        jnp.zeros((block_count * row_count, feat_width), jnp.bfloat16),
    )
    q_acc, k_acc, v_acc = lax.fori_loop(0, head_count, per_head, start_state)
    shaped = (block_count, row_count, feat_width)
    return (q_acc, k_acc.reshape(shaped), v_acc.reshape(shaped))


def adapter_gradient_list(
    inputs, projection_gradients, adapter_down_weight, adapter_up_weight, norm_scale_factor
):
    input_gradient = jnp.zeros((inputs.shape[0], inputs.shape[1]), jnp.float32)
    downs = []
    ups = []
    for projection_choice in range(3):
        output_projection = projection_gradients[projection_choice].astype(jnp.bfloat16)
        lowrank_projection = jnp.dot(
            inputs, adapter_down_weight[projection_choice], preferred_element_type=jnp.float32
        ).astype(jnp.bfloat16)
        ups.append(
            jnp.dot(lowrank_projection.T, output_projection, preferred_element_type=jnp.float32)
            * norm_scale_factor
        )
        backward_projection = jnp.dot(
            output_projection,
            adapter_up_weight[projection_choice].T,
            preferred_element_type=jnp.float32,
        ).astype(jnp.bfloat16)
        downs.append(
            jnp.dot(inputs.T, backward_projection, preferred_element_type=jnp.float32)
            * norm_scale_factor
        )
        input_gradient = input_gradient + jnp.dot(
            backward_projection,
            adapter_down_weight[projection_choice].T,
            preferred_element_type=jnp.float32,
        )
    return (input_gradient, jnp.stack(downs), jnp.stack(ups))


def per_device(
    inputs,
    queries,
    keys,
    values,
    output_gradient,
    radial_block_mask,
    adapter_down_weight,
    adapter_up_weight,
):
    axis_size = lax.axis_size("frame")
    my_block = lax.axis_index("frame")
    level_count = axis_size.bit_length() - 1
    offsets = [direction * 2**level for level in range(level_count) for direction in (1, -1)]
    received = {}
    for offset in offsets:
        received[offset] = passed_along((keys, values), "frame", offset)
    key_blocks = jnp.stack([keys] + [received[offset][0] for offset in offsets])
    val_blocks = jnp.stack([values] + [received[offset][1] for offset in offsets])
    mask_row = radial_block_mask[my_block]
    keep_list = []
    for offset in [0] + offsets:
        target = my_block - offset
        inside = (target >= 0) & (target < axis_size)
        clipped = jnp.clip(target, 0, axis_size - 1)
        keep_list.append(jnp.where(inside, mask_row[clipped], 0).astype(jnp.float32))
    query_gradient, key_parts, val_parts = block_grads(
        queries, output_gradient, key_blocks, val_blocks, jnp.stack(keep_list)
    )
    key_gradient = key_parts[0].astype(jnp.float32)
    value_gradient = val_parts[0].astype(jnp.float32)
    for position in range(len(offsets)):
        offset = offsets[position]
        back_key, back_val = passed_along(
            (key_parts[position + 1], val_parts[position + 1]), "frame", -offset
        )
        key_gradient = key_gradient + back_key.astype(jnp.float32)
        value_gradient = value_gradient + back_val.astype(jnp.float32)
    norm_scale_factor = 1.0 / math.sqrt(queries.shape[0] * axis_size)
    input_gradient, down_terms, up_terms = adapter_gradient_list(
        inputs,
        (query_gradient, key_gradient, value_gradient),
        adapter_down_weight,
        adapter_up_weight,
        norm_scale_factor,
    )
    down_gradient, up_gradient = lax.psum((down_terms, up_terms), "frame")
    return (input_gradient.astype(jnp.bfloat16), down_gradient, up_gradient)


def solution(mesh):
    in_specs = (
        P("frame", None),
        P("frame", None),
        P("frame", None),
        P("frame", None),
        P("frame", None),
        P(),
        P(),
        P(),
    )
    out_specs = (P("frame", None), P(), P())
    return jax.shard_map(
        per_device, mesh=mesh, in_specs=in_specs, out_specs=out_specs, check_vma=False
    )
```

profile of v0, /device:TPU:1, one launch (start us, length us, event | category | flops | bytes accessed | tf_op | source)
XLA Modules:
  0.0 844.3 jit_solution(5328562142844860991)
XLA Ops:
  8.7 5.0 collective-permute-start.10
  15.0 2.9 collective-permute-start.1
  17.9 3.2 collective-permute-start
  36.4 3.2 collective-permute-start.2
  44.8 7.7 collective-permute-done.2
  52.5 5.6 collective-permute-start.4
  61.2 21.8 %collective-permute-done.4 = bf16[192,1536]{1,0:T(8,128)(2,1)S(1)} collective-permute-done((bf16[192,1536]{1,0:T(8,128)(2,1)S(1)}, bf16[192,1536]{1,0:T(8,128)(2,1)S(1)}, u32[]{:S(2)}, u32[]{:S(2)}) %collective-permute-start.4) | collective-permute-done | bytes 589856 | tf_op jit(solution)/shard_map/ppermute | solution.py:14
  83.0 3.1 collective-permute-start.6
  91.9 5.5 collective-permute-done.6
  97.4 4.7 collective-permute-start.8
  106.7 6.0 collective-permute-done.8
  112.8 11.7 %collective-permute-start.12 = (bf16[192,1536]{1,0:T(8,128)(2,1)S(1)}, bf16[192,1536]{1,0:T(8,128)(2,1)S(1)}, u32[]{:S(2)}, u32[]{:S(2)}) collective-permute-start(bf16[192,1536]{1,0:T(8,128)(2,1)S(1)} %copy-done.16), channel_id=1, source_target_pairs={{0,64},{1,65},{2,66},{3,67},{4,68},{5,69},{6,70},{7,71},{8,72},{9,... | collective-permute-start | bytes 1769480 | tf_op jit(solution)/shard_map/ppermute | solution.py:14
  127.5 4.0 collective-permute-start.24
  134.5 13.8 %collective-permute-start.14 = (bf16[192,1536]{1,0:T(8,128)(2,1)S(1)}, bf16[192,1536]{1,0:T(8,128)(2,1)S(1)}, u32[]{:S(2)}, u32[]{:S(2)}) collective-permute-start(bf16[192,1536]{1,0:T(8,128)(2,1)S(1)} %copy-done.17), channel_id=1, source_target_pairs={{0,1},{1,2},{2,3},{3,4},{4,5},{5,6},{6,7},{7,8},{8,9},{9,10},{10,1... | collective-permute-start | bytes 1769480 | tf_op jit(solution)/shard_map/ppermute | solution.py:14
  152.0 3.1 collective-permute-done.14
  155.2 6.9 collective-permute-start.16
  165.1 8.1 collective-permute-done.16
  173.2 3.3 collective-permute-start.18
  177.4 3.8 collective-permute-done.17
  185.6 8.1 collective-permute-start.20
  194.6 16.2 %collective-permute-done.19 = bf16[192,1536]{1,0:T(8,128)(2,1)S(1)} collective-permute-done((bf16[192,1536]{1,0:T(8,128)(2,1)S(1)}, bf16[192,1536]{1,0:T(8,128)(2,1)S(1)}, u32[]{:S(2)}, u32[]{:S(2)}) %collective-permute-start.19) | collective-permute-done | bytes 589856 | tf_op jit(solution)/shard_map/ppermute | solution.py:14
  215.2 11.9 %collective-permute-done.21 = bf16[192,1536]{1,0:T(8,128)(2,1)S(1)} collective-permute-done((bf16[192,1536]{1,0:T(8,128)(2,1)S(1)}, bf16[192,1536]{1,0:T(8,128)(2,1)S(1)}, u32[]{:S(2)}, u32[]{:S(2)}) %collective-permute-start.21) | collective-permute-done | bytes 589856 | tf_op jit(solution)/shard_map/ppermute | solution.py:14
  229.2 37.3 %collective-permute-start.26 = (bf16[192,1536]{1,0:T(8,128)(2,1)S(1)}, bf16[192,1536]{1,0:T(8,128)(2,1)S(1)}, u32[]{:S(2)}, u32[]{:S(2)}) collective-permute-start(bf16[192,1536]{1,0:T(8,128)(2,1)S(1)} %copy-done.17), channel_id=1, source_target_pairs={{0,64},{1,65},{2,66},{3,67},{4,68},{5,69},{6,70},{7,71},{8,72},{9,... | collective-permute-start | bytes 1769480 | tf_op jit(solution)/shard_map/ppermute | solution.py:14
  270.1 7.1 collective-permute-done.26
  279.0 4.0 broadcast.65.clone
  283.1 4.1 broadcast.65
  287.3 147.0 %while.19 = (s32[]{:T(128)}, bf16[192,1536]{1,0:T(8,128)(2,1)S(1)}, bf16[2880,1536]{1,0:T(8,128)(2,1)}, bf16[2880,1536]{1,0:T(8,128)(2,1)}, bf16[192,1536]{1,0:T...) while((s32[]{:T(128)}, bf16[192,1536]{1,0:T(8,128)(2,1)S(1)}, ...), condition=%wide.region_4.5_spmd.clone, body=%wide.region_0.0_spmd.clone.sunk | while | flops 857782080 | bytes 19230408 | solution.py:58
  434.3 4.0 fusion.62
  438.4 5.0 collective-permute-start.42
  453.9 18.4 %collective-permute-done.54 = bf16[192,1536]{1,0:T(8,128)(2,1)} collective-permute-done((bf16[192,1536]{1,0:T(8,128)(2,1)S(1)}, bf16[192,1536]{1,0:T(8,128)(2,1)}, u32[]{:S(2)}, u32[]{:S(2)}) %collective-permute-start.54) | collective-permute-done | bytes 589856 | tf_op jit(solution)/shard_map/ppermute | solution.py:14
  472.3 4.8 collective-permute-start.49
  478.4 7.3 collective-permute-start.47
  492.1 7.2 collective-permute-start.43
  502.0 7.8 collective-permute-done.47
  509.8 23.6 %collective-permute-start.55 = (bf16[192,1536]{1,0:T(8,128)(2,1)S(1)}, bf16[192,1536]{1,0:T(8,128)(2,1)S(1)}, u32[]{:S(2)}, u32[]{:S(2)}) collective-permute-start(bf16[192,1536]{1,0:T(8,128)(2,1)S(1)} %get-tuple-element.300), channel_id=1, source_target_pairs={{0,64},{1,65},{2,66},{3,67},{4,68},{5,69},{6,70},{7,71},{8,72},{9,... | collective-permute-start | bytes 1769480 | tf_op jit(solution)/shard_map/ppermute | solution.py:14
  533.4 4.8 collective-permute-start.28
  539.6 3.6 collective-permute-start.39
  544.5 9.9 %collective-permute-done.55 = bf16[192,1536]{1,0:T(8,128)(2,1)S(1)} collective-permute-done((bf16[192,1536]{1,0:T(8,128)(2,1)S(1)}, bf16[192,1536]{1,0:T(8,128)(2,1)S(1)}, u32[]{:S(2)}, u32[]{:S(2)}) %collective-permute-start.55) | collective-permute-done | bytes 589856 | tf_op jit(solution)/shard_map/ppermute | solution.py:14
  557.8 15.9 %collective-permute-done.40 = bf16[192,1536]{1,0:T(8,128)(2,1)S(1)} collective-permute-done((bf16[192,1536]{1,0:T(8,128)(2,1)S(1)}, bf16[192,1536]{1,0:T(8,128)(2,1)S(1)}, u32[]{:S(2)}, u32[]{:S(2)}) %collective-permute-start.40) | collective-permute-done | bytes 589856 | tf_op jit(solution)/shard_map/ppermute | solution.py:14
  577.1 15.3 %collective-permute-start.33 = (bf16[192,1536]{1,0:T(8,128)(2,1)}, bf16[192,1536]{1,0:T(8,128)(2,1)}, u32[]{:S(2)}, u32[]{:S(2)}) collective-permute-start(bf16[192,1536]{1,0:T(8,128)(2,1)} %get-tuple-element.309), channel_id=1, source_target_pairs={{0,4},{1,5},{2,6},{3,7},{4,8},{5,9},{6,10},{7,11},{8,12},{9,13},{1... | collective-permute-start | bytes 1769480 | tf_op jit(solution)/shard_map/ppermute | solution.py:14
  597.2 3.1 collective-permute-start.31
  601.6 8.4 collective-permute-start.29
  611.8 31.0 %collective-permute-start.41 = (bf16[192,1536]{1,0:T(8,128)(2,1)}, bf16[192,1536]{1,0:T(8,128)(2,1)}, u32[]{:S(2)}, u32[]{:S(2)}) collective-permute-start(bf16[192,1536]{1,0:T(8,128)(2,1)} %get-tuple-element.314), channel_id=1, source_target_pairs={{0,64},{1,65},{2,66},{3,67},{4,68},{5,69},{6,70},{7,71},{8,72},{9,... | collective-permute-start | bytes 1769480 | tf_op jit(solution)/shard_map/ppermute | solution.py:14
  642.7 4.6 add_convert_fusion
  650.2 6.5 collective-permute-done.41
  656.7 4.6 add_convert_fusion.1
  670.5 162.5 %all-reduce.3.cloned.1.call-done = (f32[3,3072,64]{1,2,0:T(8,128)}, f32[3,64,1536]{2,1,0:T(8,128)}) async-done(((f32[3,3072,64]{1,2,0:T(8,128)}, f32[3,64,1536]{2,1,0:T(8,128)}), (f32[3,3072,64]{1,2,0:T(8,128)}, f32[3,64,1536]{2,1,0:T(8,128)})) %all-reduce.3.cloned.1.call-update) | async-done | bytes 3538960 | tf_op jit(solution)/shard_map/psum | solution.py:141
  833.0 3.4 copy.56
  (301 shorter events, 255.2 us)
Async XLA Ops:
  7.2 825.8 %all-reduce.3.cloned.1.call-start = ((), (), s32[]{:S(2)}) async-start(), calls=%async_computation | async-start | bytes 7077888 | tf_op jit(solution)/shard_map/psum | solution.py:141
  7.2 125.1 %collective-permute-start.11 = (bf16[192,1536]{1,0:T(8,128)(2,1)}, bf16[192,1536]{1,0:T(8,128)(2,1)S(1)}, u32[]{:S(2)}, u32[]{:S(2)}) collective-permute-start(bf16[192,1536]{1,0:T(8,128)(2,1)} %param.14), channel_id=1, source_target_pairs={{32,0},{33,1},{34,2},{35,3},{36,4},{37,5},{38,6},{39,7},{40,8},{41... | collective-permute-start | bytes 1769480 | tf_op jit(solution)/shard_map/ppermute | solution.py:14
  8.7 118.8 %collective-permute-start.10 = (bf16[192,1536]{1,0:T(8,128)(2,1)}, bf16[192,1536]{1,0:T(8,128)(2,1)S(1)}, u32[]{:S(2)}, u32[]{:S(2)}) collective-permute-start(bf16[192,1536]{1,0:T(8,128)(2,1)} %param.14), channel_id=1, source_target_pairs={{0,32},{1,33},{2,34},{3,35},{4,36},{5,37},{6,38},{7,39},{8,40},{9,... | collective-permute-start | bytes 1769480 | tf_op jit(solution)/shard_map/ppermute | solution.py:14
  13.7 111.6 %collective-permute-start.9 = (bf16[192,1536]{1,0:T(8,128)(2,1)}, bf16[192,1536]{1,0:T(8,128)(2,1)S(1)}, u32[]{:S(2)}, u32[]{:S(2)}) collective-permute-start(bf16[192,1536]{1,0:T(8,128)(2,1)} %param.14), channel_id=1, source_target_pairs={{16,0},{17,1},{18,2},{19,3},{20,4},{21,5},{22,6},{23,7},{24,8},{25... | collective-permute-start | bytes 1769480 | tf_op jit(solution)/shard_map/ppermute | solution.py:14
  15.0 26.6 %collective-permute-start.1 = (bf16[192,1536]{1,0:T(8,128)(2,1)}, bf16[192,1536]{1,0:T(8,128)(2,1)}, u32[]{:S(2)}, u32[]{:S(2)}) collective-permute-start(bf16[192,1536]{1,0:T(8,128)(2,1)} %param.14), channel_id=1, source_target_pairs={{1,0},{2,1},{3,2},{4,3},{5,4},{6,5},{7,6},{8,7},{9,8},{10,9},{11,1... | collective-permute-start | bytes 1769480 | tf_op jit(solution)/shard_map/ppermute | solution.py:14
  17.9 18.5 %collective-permute-start = (bf16[192,1536]{1,0:T(8,128)(2,1)}, bf16[192,1536]{1,0:T(8,128)(2,1)}, u32[]{:S(2)}, u32[]{:S(2)}) collective-permute-start(bf16[192,1536]{1,0:T(8,128)(2,1)} %param.14), channel_id=1, source_target_pairs={{0,1},{1,2},{2,3},{3,4},{4,5},{5,6},{6,7},{7,8},{8,9},{9,10},{10,1... | collective-permute-start | bytes 1769480 | tf_op jit(solution)/shard_map/ppermute | solution.py:14
  41.6 17.4 %collective-permute-start.3 = (bf16[192,1536]{1,0:T(8,128)(2,1)S(1)}, bf16[192,1536]{1,0:T(8,128)(2,1)S(1)}, u32[]{:S(2)}, u32[]{:S(2)}) collective-permute-start(bf16[192,1536]{1,0:T(8,128)(2,1)S(1)} %copy-done.16), channel_id=1, source_target_pairs={{2,0},{3,1},{4,2},{5,3},{6,4},{7,5},{8,6},{9,7},{10,8},{11,9},{12,... | collective-permute-start | bytes 1769480 | tf_op jit(solution)/shard_map/ppermute | solution.py:14
  52.5 30.5 %collective-permute-start.4 = (bf16[192,1536]{1,0:T(8,128)(2,1)S(1)}, bf16[192,1536]{1,0:T(8,128)(2,1)S(1)}, u32[]{:S(2)}, u32[]{:S(2)}) collective-permute-start(bf16[192,1536]{1,0:T(8,128)(2,1)S(1)} %copy-done.16), channel_id=1, source_target_pairs={{0,4},{1,5},{2,6},{3,7},{4,8},{5,9},{6,10},{7,11},{8,12},{9,13},{1... | collective-permute-start | bytes 1769480 | tf_op jit(solution)/shard_map/ppermute | solution.py:14
  59.0 30.7 %collective-permute-start.5 = (bf16[192,1536]{1,0:T(8,128)(2,1)S(1)}, bf16[192,1536]{1,0:T(8,128)(2,1)S(1)}, u32[]{:S(2)}, u32[]{:S(2)}) collective-permute-start(bf16[192,1536]{1,0:T(8,128)(2,1)S(1)} %copy-done.16), channel_id=1, source_target_pairs={{4,0},{5,1},{6,2},{7,3},{8,4},{9,5},{10,6},{11,7},{12,8},{13,9},{1... | collective-permute-start | bytes 1769480 | tf_op jit(solution)/shard_map/ppermute | solution.py:14
  104.6 44.6 %collective-permute-start.13 = (bf16[192,1536]{1,0:T(8,128)(2,1)S(1)}, bf16[192,1536]{1,0:T(8,128)(2,1)S(1)}, u32[]{:S(2)}, u32[]{:S(2)}) collective-permute-start(bf16[192,1536]{1,0:T(8,128)(2,1)S(1)} %copy-done.16), channel_id=1, source_target_pairs={{64,0},{65,1},{66,2},{67,3},{68,4},{69,5},{70,6},{71,7},{72,8},{73... | collective-permute-start | bytes 1769480 | tf_op jit(solution)/shard_map/ppermute | solution.py:14
  112.8 21.8 %collective-permute-start.12 = (bf16[192,1536]{1,0:T(8,128)(2,1)S(1)}, bf16[192,1536]{1,0:T(8,128)(2,1)S(1)}, u32[]{:S(2)}, u32[]{:S(2)}) collective-permute-start(bf16[192,1536]{1,0:T(8,128)(2,1)S(1)} %copy-done.16), channel_id=1, source_target_pairs={{0,64},{1,65},{2,66},{3,67},{4,68},{5,69},{6,70},{7,71},{8,72},{9,... | collective-permute-start | bytes 1769480 | tf_op jit(solution)/shard_map/ppermute | solution.py:14
  125.3 143.9 %collective-permute-start.25 = (bf16[192,1536]{1,0:T(8,128)(2,1)S(1)}, bf16[192,1536]{1,0:T(8,128)(2,1)S(1)}, u32[]{:S(2)}, u32[]{:S(2)}) collective-permute-start(bf16[192,1536]{1,0:T(8,128)(2,1)S(1)} %copy-done.17), channel_id=1, source_target_pairs={{32,0},{33,1},{34,2},{35,3},{36,4},{37,5},{38,6},{39,7},{40,8},{41... | collective-permute-start | bytes 1769480 | tf_op jit(solution)/shard_map/ppermute | solution.py:14
  127.5 140.8 %collective-permute-start.24 = (bf16[192,1536]{1,0:T(8,128)(2,1)S(1)}, bf16[192,1536]{1,0:T(8,128)(2,1)S(1)}, u32[]{:S(2)}, u32[]{:S(2)}) collective-permute-start(bf16[192,1536]{1,0:T(8,128)(2,1)S(1)} %copy-done.17), channel_id=1, source_target_pairs={{0,32},{1,33},{2,34},{3,35},{4,36},{5,37},{6,38},{7,39},{8,40},{9,... | collective-permute-start | bytes 1769480 | tf_op jit(solution)/shard_map/ppermute | solution.py:14
  132.4 135.1 %collective-permute-start.23 = (bf16[192,1536]{1,0:T(8,128)(2,1)S(1)}, bf16[192,1536]{1,0:T(8,128)(2,1)S(1)}, u32[]{:S(2)}, u32[]{:S(2)}) collective-permute-start(bf16[192,1536]{1,0:T(8,128)(2,1)S(1)} %copy-done.17), channel_id=1, source_target_pairs={{16,0},{17,1},{18,2},{19,3},{20,4},{21,5},{22,6},{23,7},{24,8},{25... | collective-permute-start | bytes 1769480 | tf_op jit(solution)/shard_map/ppermute | solution.py:14
  134.5 20.6 %collective-permute-start.14 = (bf16[192,1536]{1,0:T(8,128)(2,1)S(1)}, bf16[192,1536]{1,0:T(8,128)(2,1)S(1)}, u32[]{:S(2)}, u32[]{:S(2)}) collective-permute-start(bf16[192,1536]{1,0:T(8,128)(2,1)S(1)} %copy-done.17), channel_id=1, source_target_pairs={{0,1},{1,2},{2,3},{3,4},{4,5},{5,6},{6,7},{7,8},{8,9},{9,10},{10,1... | collective-permute-start | bytes 1769480 | tf_op jit(solution)/shard_map/ppermute | solution.py:14
  155.2 18.1 %collective-permute-start.16 = (bf16[192,1536]{1,0:T(8,128)(2,1)S(1)}, bf16[192,1536]{1,0:T(8,128)(2,1)S(1)}, u32[]{:S(2)}, u32[]{:S(2)}) collective-permute-start(bf16[192,1536]{1,0:T(8,128)(2,1)S(1)} %copy-done.17), channel_id=1, source_target_pairs={{0,2},{1,3},{2,4},{3,5},{4,6},{5,7},{6,8},{7,9},{8,10},{9,11},{10,... | collective-permute-start | bytes 1769480 | tf_op jit(solution)/shard_map/ppermute | solution.py:14
  162.9 18.3 %collective-permute-start.17 = (bf16[192,1536]{1,0:T(8,128)(2,1)S(1)}, bf16[192,1536]{1,0:T(8,128)(2,1)S(1)}, u32[]{:S(2)}, u32[]{:S(2)}) collective-permute-start(bf16[192,1536]{1,0:T(8,128)(2,1)S(1)} %copy-done.17), channel_id=1, source_target_pairs={{2,0},{3,1},{4,2},{5,3},{6,4},{7,5},{8,6},{9,7},{10,8},{11,9},{12,... | collective-permute-start | bytes 1769480 | tf_op jit(solution)/shard_map/ppermute | solution.py:14
  181.3 29.5 %collective-permute-start.19 = (bf16[192,1536]{1,0:T(8,128)(2,1)S(1)}, bf16[192,1536]{1,0:T(8,128)(2,1)S(1)}, u32[]{:S(2)}, u32[]{:S(2)}) collective-permute-start(bf16[192,1536]{1,0:T(8,128)(2,1)S(1)} %copy-done.17), channel_id=1, source_target_pairs={{4,0},{5,1},{6,2},{7,3},{8,4},{9,5},{10,6},{11,7},{12,8},{13,9},{1... | collective-permute-start | bytes 1769480 | tf_op jit(solution)/shard_map/ppermute | solution.py:14
  185.6 27.4 %collective-permute-start.20 = (bf16[192,1536]{1,0:T(8,128)(2,1)S(1)}, bf16[192,1536]{1,0:T(8,128)(2,1)S(1)}, u32[]{:S(2)}, u32[]{:S(2)}) collective-permute-start(bf16[192,1536]{1,0:T(8,128)(2,1)S(1)} %copy-done.17), channel_id=1, source_target_pairs={{0,8},{1,9},{2,10},{3,11},{4,12},{5,13},{6,14},{7,15},{8,16},{9,17... | collective-permute-start | bytes 1769480 | tf_op jit(solution)/shard_map/ppermute | solution.py:14
  210.8 16.3 %collective-permute-start.21 = (bf16[192,1536]{1,0:T(8,128)(2,1)S(1)}, bf16[192,1536]{1,0:T(8,128)(2,1)S(1)}, u32[]{:S(2)}, u32[]{:S(2)}) collective-permute-start(bf16[192,1536]{1,0:T(8,128)(2,1)S(1)} %copy-done.17), channel_id=1, source_target_pairs={{8,0},{9,1},{10,2},{11,3},{12,4},{13,5},{14,6},{15,7},{16,8},{17,9... | collective-permute-start | bytes 1769480 | tf_op jit(solution)/shard_map/ppermute | solution.py:14
  227.1 51.0 %collective-permute-start.27 = (bf16[192,1536]{1,0:T(8,128)(2,1)S(1)}, bf16[192,1536]{1,0:T(8,128)(2,1)S(1)}, u32[]{:S(2)}, u32[]{:S(2)}) collective-permute-start(bf16[192,1536]{1,0:T(8,128)(2,1)S(1)} %copy-done.17), channel_id=1, source_target_pairs={{64,0},{65,1},{66,2},{67,3},{68,4},{69,5},{70,6},{71,7},{72,8},{73... | collective-permute-start | bytes 1769480 | tf_op jit(solution)/shard_map/ppermute | solution.py:14
  229.2 47.9 %collective-permute-start.26 = (bf16[192,1536]{1,0:T(8,128)(2,1)S(1)}, bf16[192,1536]{1,0:T(8,128)(2,1)S(1)}, u32[]{:S(2)}, u32[]{:S(2)}) collective-permute-start(bf16[192,1536]{1,0:T(8,128)(2,1)S(1)} %copy-done.17), channel_id=1, source_target_pairs={{0,64},{1,65},{2,66},{3,67},{4,68},{5,69},{6,70},{7,71},{8,72},{9,... | collective-permute-start | bytes 1769480 | tf_op jit(solution)/shard_map/ppermute | solution.py:14
  443.4 28.9 %collective-permute-start.54 = (bf16[192,1536]{1,0:T(8,128)(2,1)S(1)}, bf16[192,1536]{1,0:T(8,128)(2,1)}, u32[]{:S(2)}, u32[]{:S(2)}) collective-permute-start(bf16[192,1536]{1,0:T(8,128)(2,1)S(1)} %get-tuple-element.288), channel_id=1, source_target_pairs={{64,0},{65,1},{66,2},{67,3},{68,4},{69,5},{70,6},{71,7},{72,8},{73... | collective-permute-start | bytes 1769480 | tf_op jit(solution)/shard_map/ppermute | solution.py:14
  444.7 32.4 %collective-permute-start.53 = (bf16[192,1536]{1,0:T(8,128)(2,1)S(1)}, bf16[192,1536]{1,0:T(8,128)(2,1)}, u32[]{:S(2)}, u32[]{:S(2)}) collective-permute-start(bf16[192,1536]{1,0:T(8,128)(2,1)S(1)} %get-tuple-element.289), channel_id=1, source_target_pairs={{0,32},{1,33},{2,34},{3,35},{4,36},{5,37},{6,38},{7,39},{8,40},{9,... | collective-permute-start | bytes 1769480 | tf_op jit(solution)/shard_map/ppermute | solution.py:14
  446.8 31.5 %collective-permute-start.52 = (bf16[192,1536]{1,0:T(8,128)(2,1)S(1)}, bf16[192,1536]{1,0:T(8,128)(2,1)}, u32[]{:S(2)}, u32[]{:S(2)}) collective-permute-start(bf16[192,1536]{1,0:T(8,128)(2,1)S(1)} %get-tuple-element.290), channel_id=1, source_target_pairs={{32,0},{33,1},{34,2},{35,3},{36,4},{37,5},{38,6},{39,7},{40,8},{41... | collective-permute-start | bytes 1769480 | tf_op jit(solution)/shard_map/ppermute | solution.py:14
  448.1 37.6 %collective-permute-start.51 = (bf16[192,1536]{1,0:T(8,128)(2,1)S(1)}, bf16[192,1536]{1,0:T(8,128)(2,1)}, u32[]{:S(2)}, u32[]{:S(2)}) collective-permute-start(bf16[192,1536]{1,0:T(8,128)(2,1)S(1)} %get-tuple-element.291), channel_id=1, source_target_pairs={{0,16},{1,17},{2,18},{3,19},{4,20},{5,21},{6,22},{7,23},{8,24},{9,... | collective-permute-start | bytes 1769480 | tf_op jit(solution)/shard_map/ppermute | solution.py:14
  452.6 34.6 %collective-permute-start.50 = (bf16[192,1536]{1,0:T(8,128)(2,1)S(1)}, bf16[192,1536]{1,0:T(8,128)(2,1)}, u32[]{:S(2)}, u32[]{:S(2)}) collective-permute-start(bf16[192,1536]{1,0:T(8,128)(2,1)S(1)} %get-tuple-element.292), channel_id=1, source_target_pairs={{16,0},{17,1},{18,2},{19,3},{20,4},{21,5},{22,6},{23,7},{24,8},{25... | collective-permute-start | bytes 1769480 | tf_op jit(solution)/shard_map/ppermute | solution.py:14
  472.3 16.3 %collective-permute-start.49 = (bf16[192,1536]{1,0:T(8,128)(2,1)S(1)}, bf16[192,1536]{1,0:T(8,128)(2,1)}, u32[]{:S(2)}, u32[]{:S(2)}) collective-permute-start(bf16[192,1536]{1,0:T(8,128)(2,1)S(1)} %get-tuple-element.293), channel_id=1, source_target_pairs={{0,8},{1,9},{2,10},{3,11},{4,12},{5,13},{6,14},{7,15},{8,16},{9,17... | collective-permute-start | bytes 1769480 | tf_op jit(solution)/shard_map/ppermute | solution.py:14
  478.4 31.4 %collective-permute-start.47 = (bf16[192,1536]{1,0:T(8,128)(2,1)S(1)}, bf16[192,1536]{1,0:T(8,128)(2,1)S(1)}, u32[]{:S(2)}, u32[]{:S(2)}) collective-permute-start(bf16[192,1536]{1,0:T(8,128)(2,1)S(1)} %get-tuple-element.295), channel_id=1, source_target_pairs={{0,4},{1,5},{2,6},{3,7},{4,8},{5,9},{6,10},{7,11},{8,12},{9,13},{1... | collective-permute-start | bytes 1769480 | tf_op jit(solution)/shard_map/ppermute | solution.py:14
  485.7 47.7 %collective-permute-start.46 = (bf16[192,1536]{1,0:T(8,128)(2,1)S(1)}, bf16[192,1536]{1,0:T(8,128)(2,1)S(1)}, u32[]{:S(2)}, u32[]{:S(2)}) collective-permute-start(bf16[192,1536]{1,0:T(8,128)(2,1)S(1)} %get-tuple-element.296), channel_id=1, source_target_pairs={{4,0},{5,1},{6,2},{7,3},{8,4},{9,5},{10,6},{11,7},{12,8},{13,9},{1... | collective-permute-start | bytes 1769480 | tf_op jit(solution)/shard_map/ppermute | solution.py:14
  487.2 51.0 %collective-permute-start.45 = (bf16[192,1536]{1,0:T(8,128)(2,1)S(1)}, bf16[192,1536]{1,0:T(8,128)(2,1)S(1)}, u32[]{:S(2)}, u32[]{:S(2)}) collective-permute-start(bf16[192,1536]{1,0:T(8,128)(2,1)S(1)} %get-tuple-element.297), channel_id=1, source_target_pairs={{0,2},{1,3},{2,4},{3,5},{4,6},{5,7},{6,8},{7,9},{8,10},{9,11},{10,... | collective-permute-start | bytes 1769480 | tf_op jit(solution)/shard_map/ppermute | solution.py:14
  488.6 51.0 %collective-permute-start.44 = (bf16[192,1536]{1,0:T(8,128)(2,1)S(1)}, bf16[192,1536]{1,0:T(8,128)(2,1)S(1)}, u32[]{:S(2)}, u32[]{:S(2)}) collective-permute-start(bf16[192,1536]{1,0:T(8,128)(2,1)S(1)} %get-tuple-element.298), channel_id=1, source_target_pairs={{2,0},{3,1},{4,2},{5,3},{6,4},{7,5},{8,6},{9,7},{10,8},{11,9},{12,... | collective-permute-start | bytes 1769480 | tf_op jit(solution)/shard_map/ppermute | solution.py:14
  492.1 51.1 %collective-permute-start.43 = (bf16[192,1536]{1,0:T(8,128)(2,1)S(1)}, bf16[192,1536]{1,0:T(8,128)(2,1)S(1)}, u32[]{:S(2)}, u32[]{:S(2)}) collective-permute-start(bf16[192,1536]{1,0:T(8,128)(2,1)S(1)} %get-tuple-element.299), channel_id=1, source_target_pairs={{0,1},{1,2},{2,3},{3,4},{4,5},{5,6},{6,7},{7,8},{8,9},{9,10},{10,1... | collective-permute-start | bytes 1769480 | tf_op jit(solution)/shard_map/ppermute | solution.py:14
  509.8 44.6 %collective-permute-start.55 = (bf16[192,1536]{1,0:T(8,128)(2,1)S(1)}, bf16[192,1536]{1,0:T(8,128)(2,1)S(1)}, u32[]{:S(2)}, u32[]{:S(2)}) collective-permute-start(bf16[192,1536]{1,0:T(8,128)(2,1)S(1)} %get-tuple-element.300), channel_id=1, source_target_pairs={{0,64},{1,65},{2,66},{3,67},{4,68},{5,69},{6,70},{7,71},{8,72},{9,... | collective-permute-start | bytes 1769480 | tf_op jit(solution)/shard_map/ppermute | solution.py:14
  533.4 23.1 %collective-permute-start.28 = (bf16[192,1536]{1,0:T(8,128)(2,1)S(1)}, bf16[192,1536]{1,0:T(8,128)(2,1)S(1)}, u32[]{:S(2)}, u32[]{:S(2)}) collective-permute-start(bf16[192,1536]{1,0:T(8,128)(2,1)S(1)} %get-tuple-element.301), channel_id=1, source_target_pairs={{1,0},{2,1},{3,2},{4,3},{5,4},{6,5},{7,6},{8,7},{9,8},{10,9},{11,1... | collective-permute-start | bytes 1769480 | tf_op jit(solution)/shard_map/ppermute | solution.py:14
  538.2 35.5 %collective-permute-start.40 = (bf16[192,1536]{1,0:T(8,128)(2,1)S(1)}, bf16[192,1536]{1,0:T(8,128)(2,1)S(1)}, u32[]{:S(2)}, u32[]{:S(2)}) collective-permute-start(bf16[192,1536]{1,0:T(8,128)(2,1)S(1)} %get-tuple-element.302), channel_id=1, source_target_pairs={{64,0},{65,1},{66,2},{67,3},{68,4},{69,5},{70,6},{71,7},{72,8},{73... | collective-permute-start | bytes 1769480 | tf_op jit(solution)/shard_map/ppermute | solution.py:14
  539.6 36.3 %collective-permute-start.39 = (bf16[192,1536]{1,0:T(8,128)(2,1)S(1)}, bf16[192,1536]{1,0:T(8,128)(2,1)S(1)}, u32[]{:S(2)}, u32[]{:S(2)}) collective-permute-start(bf16[192,1536]{1,0:T(8,128)(2,1)S(1)} %get-tuple-element.303), channel_id=1, source_target_pairs={{0,32},{1,33},{2,34},{3,35},{4,36},{5,37},{6,38},{7,39},{8,40},{9,... | collective-permute-start | bytes 1769480 | tf_op jit(solution)/shard_map/ppermute | solution.py:14
  543.2 33.9 %collective-permute-start.38 = (bf16[192,1536]{1,0:T(8,128)(2,1)S(1)}, bf16[192,1536]{1,0:T(8,128)(2,1)S(1)}, u32[]{:S(2)}, u32[]{:S(2)}) collective-permute-start(bf16[192,1536]{1,0:T(8,128)(2,1)S(1)} %get-tuple-element.304), channel_id=1, source_target_pairs={{32,0},{33,1},{34,2},{35,3},{36,4},{37,5},{38,6},{39,7},{40,8},{41... | collective-permute-start | bytes 1769480 | tf_op jit(solution)/shard_map/ppermute | solution.py:14
  554.4 41.5 %collective-permute-start.37 = (bf16[192,1536]{1,0:T(8,128)(2,1)}, bf16[192,1536]{1,0:T(8,128)(2,1)}, u32[]{:S(2)}, u32[]{:S(2)}) collective-permute-start(bf16[192,1536]{1,0:T(8,128)(2,1)} %get-tuple-element.305), channel_id=1, source_target_pairs={{0,16},{1,17},{2,18},{3,19},{4,20},{5,21},{6,22},{7,23},{8,24},{9,... | collective-permute-start | bytes 1769480 | tf_op jit(solution)/shard_map/ppermute | solution.py:14
  556.5 40.7 %collective-permute-start.36 = (bf16[192,1536]{1,0:T(8,128)(2,1)}, bf16[192,1536]{1,0:T(8,128)(2,1)}, u32[]{:S(2)}, u32[]{:S(2)}) collective-permute-start(bf16[192,1536]{1,0:T(8,128)(2,1)} %get-tuple-element.306), channel_id=1, source_target_pairs={{16,0},{17,1},{18,2},{19,3},{20,4},{21,5},{22,6},{23,7},{24,8},{25... | collective-permute-start | bytes 1769480 | tf_op jit(solution)/shard_map/ppermute | solution.py:14
  573.7 26.6 %collective-permute-start.35 = (bf16[192,1536]{1,0:T(8,128)(2,1)}, bf16[192,1536]{1,0:T(8,128)(2,1)}, u32[]{:S(2)}, u32[]{:S(2)}) collective-permute-start(bf16[192,1536]{1,0:T(8,128)(2,1)} %get-tuple-element.307), channel_id=1, source_target_pairs={{0,8},{1,9},{2,10},{3,11},{4,12},{5,13},{6,14},{7,15},{8,16},{9,17... | collective-permute-start | bytes 1769480 | tf_op jit(solution)/shard_map/ppermute | solution.py:14
  575.8 25.8 %collective-permute-start.34 = (bf16[192,1536]{1,0:T(8,128)(2,1)}, bf16[192,1536]{1,0:T(8,128)(2,1)}, u32[]{:S(2)}, u32[]{:S(2)}) collective-permute-start(bf16[192,1536]{1,0:T(8,128)(2,1)} %get-tuple-element.308), channel_id=1, source_target_pairs={{8,0},{9,1},{10,2},{11,3},{12,4},{13,5},{14,6},{15,7},{16,8},{17,9... | collective-permute-start | bytes 1769480 | tf_op jit(solution)/shard_map/ppermute | solution.py:14
  577.1 34.6 %collective-permute-start.33 = (bf16[192,1536]{1,0:T(8,128)(2,1)}, bf16[192,1536]{1,0:T(8,128)(2,1)}, u32[]{:S(2)}, u32[]{:S(2)}) collective-permute-start(bf16[192,1536]{1,0:T(8,128)(2,1)} %get-tuple-element.309), channel_id=1, source_target_pairs={{0,4},{1,5},{2,6},{3,7},{4,8},{5,9},{6,10},{7,11},{8,12},{9,13},{1... | collective-permute-start | bytes 1769480 | tf_op jit(solution)/shard_map/ppermute | solution.py:14
  595.9 54.3 %collective-permute-start.32 = (bf16[192,1536]{1,0:T(8,128)(2,1)}, bf16[192,1536]{1,0:T(8,128)(2,1)}, u32[]{:S(2)}, u32[]{:S(2)}) collective-permute-start(bf16[192,1536]{1,0:T(8,128)(2,1)} %get-tuple-element.310), channel_id=1, source_target_pairs={{4,0},{5,1},{6,2},{7,3},{8,4},{9,5},{10,6},{11,7},{12,8},{13,9},{1... | collective-permute-start | bytes 1769480 | tf_op jit(solution)/shard_map/ppermute | solution.py:14
  597.2 53.0 %collective-permute-start.31 = (bf16[192,1536]{1,0:T(8,128)(2,1)}, bf16[192,1536]{1,0:T(8,128)(2,1)}, u32[]{:S(2)}, u32[]{:S(2)}) collective-permute-start(bf16[192,1536]{1,0:T(8,128)(2,1)} %get-tuple-element.311), channel_id=1, source_target_pairs={{0,2},{1,3},{2,4},{3,5},{4,6},{5,7},{6,8},{7,9},{8,10},{9,11},{10,... | collective-permute-start | bytes 1769480 | tf_op jit(solution)/shard_map/ppermute | solution.py:14
  600.3 49.9 %collective-permute-start.30 = (bf16[192,1536]{1,0:T(8,128)(2,1)}, bf16[192,1536]{1,0:T(8,128)(2,1)}, u32[]{:S(2)}, u32[]{:S(2)}) collective-permute-start(bf16[192,1536]{1,0:T(8,128)(2,1)} %get-tuple-element.312), channel_id=1, source_target_pairs={{2,0},{3,1},{4,2},{5,3},{6,4},{7,5},{8,6},{9,7},{10,8},{11,9},{12,... | collective-permute-start | bytes 1769480 | tf_op jit(solution)/shard_map/ppermute | solution.py:14
  601.6 48.6 %collective-permute-start.29 = (bf16[192,1536]{1,0:T(8,128)(2,1)}, bf16[192,1536]{1,0:T(8,128)(2,1)}, u32[]{:S(2)}, u32[]{:S(2)}) collective-permute-start(bf16[192,1536]{1,0:T(8,128)(2,1)} %get-tuple-element.313), channel_id=1, source_target_pairs={{0,1},{1,2},{2,3},{3,4},{4,5},{5,6},{6,7},{7,8},{8,9},{9,10},{10,1... | collective-permute-start | bytes 1769480 | tf_op jit(solution)/shard_map/ppermute | solution.py:14
  611.8 44.9 %collective-permute-start.41 = (bf16[192,1536]{1,0:T(8,128)(2,1)}, bf16[192,1536]{1,0:T(8,128)(2,1)}, u32[]{:S(2)}, u32[]{:S(2)}) collective-permute-start(bf16[192,1536]{1,0:T(8,128)(2,1)} %get-tuple-element.314), channel_id=1, source_target_pairs={{0,64},{1,65},{2,66},{3,67},{4,68},{5,69},{6,70},{7,71},{8,72},{9,... | collective-permute-start | bytes 1769480 | tf_op jit(solution)/shard_map/ppermute | solution.py:14
  (44 other events, 1576.9 us)
Sparse Core Ops, SparseCore 0:
  668.1 164.8 all-reduce.2
where the time goes:
time: 849 us; the launch traced here: 844 us
  waiting for transfers between devices  325 us (38%)
  starting transfers between devices  271 us (32%)
  matrix products  153 us (18%)
  local copies, waits for them, and re-layouts  52 us (6%)
  between operations  24.5 us (3%)
  other arithmetic  18 us (2%)
    ppermute x56, starting transfers between devices, passed_along(): lax.ppermute(value, axis, [(source, source + steps) for source in range(i...  271 us
    ppermute x56, waiting for transfers between devices, passed_along(): lax.ppermute(value, axis, [(source, source + steps) for source in range(i...  163 us
    psum x1, waiting for transfers between devices, per_device(): down_gradient, up_gradient = lax.psum((down_terms, up_terms), 'frame')  163 us
    unnamed x100, local copies, waits for them, and re-layouts  33.7 us
    dot_general x12, matrix products, per_head(): jnp.dot(probs_b.T, g_head, preferred_element_type=jnp.float32)  29.9 us
    dot_general x12, matrix products, per_head(): jnp.dot(dscores.T, q_head, preferred_element_type=jnp.float32) * inv_root  28.7 us
    dot_general x12, matrix products, per_head(): attended = jnp.dot(probs_b, v_head, preferred_element_type=jnp.float32)  21.6 us
    dot_general x12, matrix products, per_head(): dprobs = jnp.dot(g_head, v_head.T, preferred_element_type=jnp.float32)  20.8 us
  transfers between devices with their start and end apart: 57, of which 22 were waited for; matrix products, arithmetic and copies ran while one was open for 6% of the time, Pallas kernels for 0%

commit v1 on v0

v1 whole, which is shorter than its diff:
```python
import functools
import math

import jax
import jax.numpy as jnp
from jax import lax
from jax.experimental import pallas as pl
from jax.experimental.pallas import tpu as pltpu
from jax.sharding import PartitionSpec as P

MESH = pl.DeviceIdType.MESH
DH = 128
HEADS = 12
TOK = 192
RANK = 64
WIDTH = 3072
FEAT = HEADS * DH
OWN, PARTNER, SIDE = 0, 1, 2
SLOT = {1: 3, -1: 4, 2: 5, -2: 6, 4: 7, -4: 8, 8: 9, -8: 10, 16: 11, -16: 12, 32: 13, -32: 14}
SLOTS = 15
VIA_Y, VIA_Z = 15, 16
KEYS = SLOTS * TOK
PAD = 3072
TILES = [(0, 512), (512, 512), (1024, 512), (1536, 512), (2048, 512), (2560, 320)]
ROOT = 1.0 / math.sqrt(DH)
MASKED = -1e30


def nt(a, b):
    return lax.dot_general(a, b, (((1,), (1,)), ((), ())), preferred_element_type=jnp.float32)


def nn(a, b):
    return lax.dot_general(a, b, (((1,), (0,)), ((), ())), preferred_element_type=jnp.float32)


def pick(cond, a, b):
    return jnp.where(cond, a, b)


def hops(d, z, x, y):
    if abs(d) == 16:
        return 1
    if d == 4:
        return pick(x == 0, 2, 1)
    if d == -4:
        return pick(x == 3, 2, 1)
    if d == 1:
        return pick(y == 0, pick(x == 0, 3, 2), 1)
    if d == -1:
        return pick(y == 3, pick(x == 3, 3, 2), 1)
    if d == 8:
        return pick(x >= 2, 2, 3)
    if d == -8:
        return pick(x <= 1, 2, 3)
    if abs(d) == 32:
        return 2
    if d == 2:
        return pick(y >= 2, 2, pick(x == 0, 4, 3))
    return pick(y <= 1, 2, pick(x == 3, 4, 3))


def attention_kernel(
    mask_ref, x_ref, q_ref, g_ref, k_ref, v_ref, down_ref, up_ref,
    back_out, upgrad_out,
    buf, lowbuf, bias, s_ref, d_ref, acc, back0, lowt0, rsend, rrecv,
    load_sem, send_sem, recv_sem, lsend, lrecv, rs_send, rs_recv,
):
    me = lax.axis_index("frame")
    i = me // 2
    c = me % 2
    z = i // 16
    x = (i // 4) % 4
    y = i % 4

    def dev(zz, xx, yy, cc):
        return ((zz + 4) % 4) * 32 + ((xx + 4) % 4) * 8 + ((yy + 4) % 4) * 2 + cc

    yp, ym = dev(z, x, y + 1, c), dev(z, x, y - 1, c)
    xp, xm = dev(z, x + 1, y, c), dev(z, x - 1, y, c)
    zp, zm = dev(z + 1, x, y, c), dev(z - 1, x, y, c)
    pt = dev(z, x, y, 1 - c)
    side = pick(c == 0, me - 1, me + 1)
    side_ok = (side >= 0) & (side < 128)

    def valid(d):
        return (i - d >= 0) & (i - d < 64)

    def rows(s):
        return pl.ds(s * TOK, TOK)

    barrier = pltpu.get_barrier_semaphore()
    for d in (yp, ym, xp, xm, zp, zm, pt):
        pl.semaphore_signal(barrier, inc=1, device_id=(d,), device_id_type=MESH)
    count = jnp.int32(7)
    for d in SLOT:
        count = count + pick(valid(d), 1, 0)

        @pl.when(valid(d))
        def _(d=d):
            pl.semaphore_signal(barrier, inc=1, device_id=(me - 2 * d,), device_id_type=MESH)

    count = count + pick(side_ok, 1, 0)

    @pl.when(side_ok)
    def _():
        pl.semaphore_signal(barrier, inc=1, device_id=(side,), device_id_type=MESH)

    def load(h, a):
        ref = (k_ref, v_ref)[a]
        return pltpu.make_async_copy(
            ref.at[:, pl.ds(h * DH, DH)], buf.at[h, a, rows(OWN)], load_sem.at[h, a]
        )

    for h in range(HEADS):
        for a in range(2):
            load(h, a).start()

    every = [(d, SLOT[d]) for d in SLOT]
    for d, s in every:
        @pl.when(jnp.logical_not(valid(d)))
        def _(s=s):
            lowbuf[rows(s), :] = jnp.zeros((TOK, DH), jnp.bfloat16)
            rrecv[s] = jnp.zeros((2 * RANK, TOK), jnp.bfloat16)

            def zero(h, _):
                for a in range(2):
                    buf[h, a, rows(s), :] = jnp.zeros((TOK, DH), jnp.bfloat16)
                return 0

            lax.fori_loop(0, HEADS, zero, 0)

    @pl.when(jnp.logical_not(side_ok))
    def _():
        lowbuf[rows(SIDE), :] = jnp.zeros((TOK, DH), jnp.bfloat16)
        rrecv[SIDE] = jnp.zeros((2 * RANK, TOK), jnp.bfloat16)

        def zero(h, _):
            for a in range(2):
                buf[h, a, rows(SIDE), :] = jnp.zeros((TOK, DH), jnp.bfloat16)
            return 0

        lax.fori_loop(0, HEADS, zero, 0)

    lane = lax.broadcasted_iota(jnp.int32, (8, PAD), 1)
    total_bias = jnp.zeros((8, PAD), jnp.float32)
    for s, (block, ok) in enumerate(
        [(me, None), (pt, None), (side, side_ok)] + [(me - 2 * d, valid(d)) for d in SLOT]
    ):
        kept = mask_ref[me, jnp.clip(block, 0, 127)]
        value = jnp.where(kept > 0, 0.0, MASKED)
        if ok is not None:
            value = jnp.where(ok, value, MASKED)
        inside = (lane >= s * TOK) & (lane < (s + 1) * TOK)
        total_bias = jnp.where(inside, value, total_bias)
    bias[...] = total_bias

    low = nt(x_ref[...], down_ref[...]).astype(jnp.bfloat16)
    lowt0[...] = nt(down_ref[0:RANK, :], x_ref[...]).astype(jnp.bfloat16)
    lowbuf[rows(OWN), :] = low[:, RANK:]
    acc[...] = jnp.zeros_like(acc)
    back0[...] = jnp.zeros_like(back0)

    def low_copy(s, device):
        return pltpu.make_async_remote_copy(
            src_ref=lowbuf.at[rows(OWN)], dst_ref=lowbuf.at[rows(s)],
            send_sem=lsend.at[s], recv_sem=lrecv.at[s],
            device_id=(device,), device_id_type=MESH,
        )

    def back_copy(s, device):
        return pltpu.make_async_remote_copy(
            src_ref=rsend.at[s], dst_ref=rrecv.at[s],
            send_sem=rs_send.at[s], recv_sem=rs_recv.at[s],
            device_id=(device,), device_id_type=MESH,
        )

    direct = [(PARTNER, None, None, pt, pt), (SIDE, side_ok, side_ok, side, side)]
    direct += [(SLOT[d], valid(-d), valid(d), me + 2 * d, me - 2 * d) for d in SLOT]

    def guarded(cond, f):
        if cond is None:
            f()
        else:
            pl.when(cond)(f)

    def copy(kind, h, src, dst, device):
        return pltpu.make_async_remote_copy(
            src_ref=buf.at[h, :, rows(src)], dst_ref=buf.at[h, :, rows(dst)],
            send_sem=send_sem.at[kind, h], recv_sem=recv_sem.at[dst, h],
            device_id=(device,), device_id_type=MESH,
        )

    kinds = []

    def kind(cond, src, dst, device):
        kinds.append((cond, src, dst, device))
        return len(kinds) - 1

    mid = (x == 1) | (x == 2)

    def by_ring_up(xx, h):
        return (xx == 0) | (((xx == 1) | (xx == 2)) & (h % 2 == 0))

    def by_ring_down(xx, h):
        return (xx == 3) | (((xx == 1) | (xx == 2)) & (h % 2 == 1))

    def late(h):
        return (h // 2) % 2 == 0

    def up_here(h):
        return by_ring_up(x, h)

    def down_here(h):
        return by_ring_down(x, h)

    def always(cond):
        return lambda h: cond

    own = [
        kind(None, OWN, PARTNER, pt),
        kind(always(y < 3), OWN, SLOT[1], yp), kind(always(y > 0), OWN, SLOT[-1], ym),
        kind(always(x < 3), OWN, SLOT[4], xp), kind(always(x > 0), OWN, SLOT[-4], xm),
        kind(always(z < 3), OWN, SLOT[16], zp), kind(always(z > 0), OWN, SLOT[-16], zm),
        kind(always((z == 0) & (x == 0)), OWN, VIA_Z, zm),
        kind(always((z == 3) & (x == 3)), OWN, VIA_Z, zp),
    ]
    on = {}
    on[16] = [
        kind(always((z == 1) & (x != 0)), SLOT[16], SLOT[32], zp),
        kind(always(z == 3), SLOT[16], SLOT[-32], zp),
        kind(always((x == 3) & (z > 0)), SLOT[16], SLOT[4], xp),
    ]
    on[-16] = [
        kind(always((z == 2) & (x != 3)), SLOT[-16], SLOT[-32], zm),
        kind(always(z == 0), SLOT[-16], SLOT[32], zm),
        kind(always((x == 0) & (z < 3)), SLOT[-16], SLOT[-4], xm),
    ]
    on["z"] = [
        kind(always((z == 3) & (x == 0)), VIA_Z, SLOT[32], zm),
        kind(always((z == 0) & (x == 3)), VIA_Z, SLOT[-32], zp),
    ]
    on[4] = [
        kind(always((x < 2) & valid(4)), SLOT[4], SLOT[8], xp),
        kind(always(x == 3), SLOT[4], SLOT[-8], xp),
        kind(always((y == 3) & valid(4)), SLOT[4], SLOT[1], yp),
        kind(lambda h: (y == 2) & valid(4) & up_here(h), SLOT[4], VIA_Y, yp),
    ]
    on[-4] = [
        kind(always((x > 1) & valid(-4)), SLOT[-4], SLOT[-8], xm),
        kind(always(x == 0), SLOT[-4], SLOT[8], xm),
        kind(always((y == 0) & valid(-4)), SLOT[-4], SLOT[-1], ym),
        kind(lambda h: (y == 1) & valid(-4) & down_here(h), SLOT[-4], VIA_Y, ym),
    ]
    on[1] = [
        kind(lambda h: valid(1) & ((y < 2) | ((y == 2) & jnp.logical_not(up_here(h)))), SLOT[1], SLOT[2], yp),
        kind(lambda h: (y == 3) & jnp.logical_not(up_here(h)), SLOT[1], SLOT[-2], yp),
        kind(always((c == 1) & valid(1)), SLOT[1], SIDE, pt),
        kind(
            lambda h: (y == 3) & (x < 3) & jnp.logical_not(by_ring_up(x + 1, h)) & jnp.logical_not(late(h)),
            SLOT[1], VIA_Y, xp,
        ),
    ]
    on[-1] = [
        kind(lambda h: valid(-1) & ((y > 1) | ((y == 1) & up_here(h))), SLOT[-1], SLOT[-2], ym),
        kind(lambda h: (y == 0) & up_here(h), SLOT[-1], SLOT[2], ym),
        kind(always((c == 0) & valid(-1)), SLOT[-1], SIDE, pt),
        kind(
            lambda h: (y == 0) & (x > 0) & jnp.logical_not(by_ring_down(x - 1, h)) & jnp.logical_not(late(h)),
            SLOT[-1], VIA_Y, xm,
        ),
    ]

    def has_via_y(h):
        up = (y == 3) & ((z > 0) | (x > 0)) & (up_here(h) | jnp.logical_not(late(h)))
        down = (y == 0) & ((z < 3) | (x < 3)) & (down_here(h) | jnp.logical_not(late(h)))
        return up | down

    via_z = ((z == 3) & (x == 0)) | ((z == 0) & (x == 3))
    on["y"] = [
        kind(lambda h: (y == 3) & has_via_y(h), VIA_Y, SLOT[2], yp),
        kind(lambda h: (y == 0) & has_via_y(h), VIA_Y, SLOT[-2], ym),
    ]
    on[2] = [
        kind(lambda h: (y == 3) & (x > 0) & jnp.logical_not(by_ring_down(x - 1, h)) & late(h), SLOT[2], SLOT[-2], xm),
    ]
    on[-2] = [
        kind(lambda h: (y == 0) & (x < 3) & jnp.logical_not(by_ring_up(x + 1, h)) & late(h), SLOT[-2], SLOT[2], xp),
    ]
    on[8] = [kind(always((x == 3) & (z > 0)), SLOT[8], SLOT[-8], zm)]
    on[-8] = [kind(always((x == 0) & (z < 3)), SLOT[-8], SLOT[8], zp)]
    on[32] = []
    on[-32] = []

    def slot_of(d):
        return VIA_Y if d == "y" else VIA_Z if d == "z" else SLOT[d]

    def comes(d, h):
        return has_via_y(h) if d == "y" else via_z if d == "z" else valid(d)

    def lag(d):
        if d == "z":
            return 1
        if d == "y":
            return pick(((y == 3) & (x == 0)) | ((y == 0) & (x == 3)), 3, 2)
        return hops(d, z, x, y)

    def send(k, h):
        cond, src, dst, device = kinds[k]
        guarded(None if cond is None else cond(h), lambda: copy(k, h, src, dst, device).start())

    def arrived(s, h):
        copy(0, h, s, s, pt).wait_recv()

    def head(h):
        cols = pl.ds(pl.multiple_of(h * DH, DH), DH)
        q = q_ref[:, cols]
        g = g_ref[:, cols]
        top = None
        for t0, w in TILES:
            kt = buf[h, 0, pl.ds(t0, w), :]
            s = nt(q, kt) * (ROOT * math.log2(math.e)) + bias[0:1, t0:t0 + w]
            s_ref[:, t0:t0 + w] = s
            m = jnp.max(s, axis=1, keepdims=True)
            top = m if top is None else jnp.maximum(top, m)
        total = jnp.zeros((TOK, 1), jnp.float32)
        dot = jnp.zeros((TOK, 1), jnp.float32)
        for t0, w in TILES:
            e = jnp.exp2(s_ref[:, t0:t0 + w] - top)
            s_ref[:, t0:t0 + w] = e
            dp = nt(g, buf[h, 1, pl.ds(t0, w), :])
            d_ref[:, t0:t0 + w] = dp
            total = total + jnp.sum(e, axis=1, keepdims=True)
            dot = dot + jnp.sum(e * dp, axis=1, keepdims=True)
        inv = 1.0 / total
        dot = dot * inv
        qu = (nt(up_ref[1, :, cols], q) * ROOT).astype(jnp.bfloat16)
        gu = nt(up_ref[2, :, cols], g).astype(jnp.bfloat16)
        both = jnp.zeros((TOK, 2 * DH), jnp.float32)
        vlow = jnp.zeros((TOK, DH), jnp.float32)
        for t0, w in TILES:
            p = s_ref[:, t0:t0 + w] * inv
            pb = p.astype(jnp.bfloat16)
            ds = (p * (d_ref[:, t0:t0 + w] - dot)).astype(jnp.bfloat16)
            kt = buf[h, 0, pl.ds(t0, w), :]
            lt = lowbuf[pl.ds(t0, w), :]
            both = both + nn(ds, jnp.concatenate([kt, lt], axis=1))
            vlow = vlow + nn(pb, lt)
            acc[0:RANK, t0:t0 + w] += nn(qu, ds)
            acc[RANK:, t0:t0 + w] += nn(gu, pb)
        out0 = (both[:, 0:DH] * ROOT).astype(jnp.bfloat16)
        klow = both[:, DH:DH + RANK] * ROOT
        upgrad_out[0, :, cols] = nn(lowt0[...], out0)
        back0[...] += nt(up_ref[0, :, cols], out0)
        lows = jnp.concatenate([klow, vlow[:, RANK:]], axis=1).T.astype(jnp.bfloat16)
        upgrad_out[1, :, cols] = nn(lows[0:RANK], q)
        upgrad_out[2, :, cols] = nn(lows[RANK:], g)

    pl.semaphore_wait(barrier, count)

    last = 4
    order = [16, -16, 4, -4, 1, -1, "z", "y", 8, -8, 2, -2, 32, -32]

    def step(r, _):
        @pl.when(r < HEADS)
        def _():
            for a in range(2):
                load(r, a).wait()
            for k in own:
                send(k, r)

        for d in order:
            h = r - lag(d)

            @pl.when((h >= 0) & (h < HEADS) & comes(d, h))
            def _(d=d, h=h):
                arrived(slot_of(d), h)
                for k in on[d]:
                    send(k, h)

        @pl.when(r == 0)
        def _():
            for s, goes, _, to, _ in direct:
                guarded(goes, low_copy(s, to).start)

        @pl.when(r == last)
        def _():
            for s, _, comes_in, _, _ in direct:
                guarded(comes_in, low_copy(s, pt).wait_recv)

        h = r - last

        @pl.when((h >= 0) & (h < HEADS))
        def _():
            arrived(PARTNER, h)

            @pl.when(((c == 0) & valid(1)) | ((c == 1) & valid(-1)))
            def _():
                arrived(SIDE, h)

            head(h)

        return 0

    lax.fori_loop(0, HEADS + last, step, 0)

    for s, _, goes, _, to in direct:
        rsend[s] = acc[:, s * TOK:(s + 1) * TOK].astype(jnp.bfloat16)
        guarded(goes, back_copy(s, to).start)
    total = acc[:, 0:TOK]
    for s, comes_in, _, _, _ in direct:
        guarded(comes_in, back_copy(s, pt).wait_recv)
        total = total + rrecv[s].astype(jnp.float32)
    back_out[0:RANK, :] = back0[...].astype(jnp.bfloat16)
    back_out[RANK:, :] = total.astype(jnp.bfloat16)

    for s, goes, returns, to, owner in direct:
        guarded(goes, low_copy(s, to).wait_send)
        guarded(returns, back_copy(s, owner).wait_send)

    def drain(h, _):
        for k, (cond, src, dst, device) in enumerate(kinds):
            guarded(
                None if cond is None else cond(h),
                lambda: copy(k, h, src, dst, device).wait_send(),
            )
        return 0

    lax.fori_loop(0, HEADS, drain, 0)


def attention(mask, inputs, queries, output_gradient, keys, values, down_t, up):
    vm = pl.BlockSpec(memory_space=pltpu.VMEM)
    dma = pltpu.SemaphoreType.DMA
    return pl.pallas_call(
        attention_kernel,
        out_shape=(
            jax.ShapeDtypeStruct((3 * RANK, TOK), jnp.bfloat16),
            jax.ShapeDtypeStruct((3, RANK, FEAT), jnp.float32),
        ),
        in_specs=[pl.BlockSpec(memory_space=pltpu.SMEM), vm, vm, vm,
                  pl.BlockSpec(memory_space=pl.ANY), pl.BlockSpec(memory_space=pl.ANY), vm, vm],
        out_specs=(vm, vm),
        scratch_shapes=[
            pltpu.VMEM((HEADS, 2, (SLOTS + 2) * TOK, DH), jnp.bfloat16),
            pltpu.VMEM((KEYS, DH), jnp.bfloat16),
            pltpu.VMEM((8, PAD), jnp.float32),
            pltpu.VMEM((TOK, PAD), jnp.float32),
            pltpu.VMEM((TOK, PAD), jnp.float32),
            pltpu.VMEM((2 * RANK, PAD), jnp.float32),
            pltpu.VMEM((RANK, TOK), jnp.float32),
            pltpu.VMEM((RANK, TOK), jnp.bfloat16),
            pltpu.VMEM((SLOTS, 2 * RANK, TOK), jnp.bfloat16),
            pltpu.VMEM((SLOTS, 2 * RANK, TOK), jnp.bfloat16),
            dma((HEADS, 2)),
            dma((39, HEADS)),
            dma((SLOTS + 2, HEADS)),
            dma((SLOTS,)), dma((SLOTS,)), dma((SLOTS,)), dma((SLOTS,)),
        ],
        compiler_params=pltpu.CompilerParams(
            collective_id=0, has_side_effects=True, vmem_limit_bytes=56 * 2**20
        ),
        cost_estimate=pl.CostEstimate(flops=12 * 10**9, bytes_accessed=8 * 10**6, transcendentals=7 * 10**6),
        name="attention_gradients",
    )(mask, inputs, queries, output_gradient, keys, values, down_t, up)


def per_device(
    inputs, queries, keys, values, output_gradient, radial_block_mask,
    adapter_down_weight, adapter_up_weight,
):
    axis_size = lax.axis_size("frame")
    norm = 1.0 / math.sqrt(TOK * axis_size)
    down_t = jnp.swapaxes(adapter_down_weight, 1, 2).reshape(3 * RANK, WIDTH)
    back, up_terms = attention(
        radial_block_mask, inputs, queries, output_gradient, keys, values, down_t, adapter_up_weight
    )
    down_terms = nn(back, inputs) * norm
    input_gradient = lax.dot_general(
        back, down_t, (((0,), (0,)), ((), ())), preferred_element_type=jnp.float32
    )
    down, up = lax.psum((down_terms, up_terms * norm), "frame")
    down = jnp.swapaxes(down.reshape(3, RANK, WIDTH), 1, 2)
    return (input_gradient.astype(jnp.bfloat16), down, up)


def solution(mesh):
    return jax.shard_map(
        per_device,
        mesh=mesh,
        in_specs=(P("frame", None),) * 5 + (P(), P(), P()),
        out_specs=(P("frame", None), P(), P()),
        check_vma=False,
    )
```

time: 849 us -> 284 us (0.33)
  starting transfers between devices: 271 us -> 0.04 us
  waiting for transfers between devices: 325 us -> 151 us
  matrix products: 153 us -> 4.38 us
  Pallas kernels: 0 us -> 108 us
  local copies, waits for them, and re-layouts: 52 us -> 5.67 us
  other arithmetic: 18 us -> 1.13 us
  between operations: 24.5 us -> 14.1 us
    ppermute x56 -> x0, starting transfers between devices: 271 us -> none  [passed_along(): lax.ppermute(value, axis, [(source, source + steps) for source in range(i...]
    ppermute x56 -> x0, waiting for transfers between devices: 163 us -> none  [passed_along(): lax.ppermute(value, axis, [(source, source + steps) for source in range(i...]
    dot_general x84 -> x2, matrix products: 153 us -> 4.38 us  [the longest x1 2.87 us: nn(): lax.dot_general(a, b, (((1,), (0,)), ((), ())), preferred_element_type=jn...]
    pallas_call x0 -> x1, Pallas kernels: none -> 108 us  [attention(): pl.pallas_call(attention_kernel, out_shape=(jax.ShapeDtypeStruct((3 * RAN...]
    unnamed x100 -> x12, local copies, waits for them, and re-layouts: 33.7 us -> 5.67 us
    psum x1, waiting for transfers between devices: 163 us -> 151 us  [per_device(): down, up = lax.psum((down_terms, up_terms * norm), 'frame')]
    another operation x4 -> x0, local copies, waits for them, and re-layouts: 9.79 us -> none
    convert_element_type x2 -> x0, other arithmetic: 9.28 us -> none  [adapter_gradient_list(): projection_gradients[projection_choice].astype(jnp.bfloat16)]
  transfers between devices with their start and end apart: 57 -> 1, of which waited for: 22 -> 1; matrix products, arithmetic and copies ran while one was open for 6% -> 1% of each run, Pallas kernels for 0% -> 0%
where the time goes in v1:
time: 284 us
  waiting for transfers between devices  151 us (53%)
  Pallas kernels  108 us (38%)
  between operations  14.1 us (5%)
  local copies, waits for them, and re-layouts  5.67 us (2%)
  matrix products  4.38 us (2%)
    psum x1, waiting for transfers between devices, per_device(): down, up = lax.psum((down_terms, up_terms * norm), 'frame')  151 us
    pallas_call x1, Pallas kernels, attention(): pl.pallas_call(attention_kernel, out_shape=(jax.ShapeDtypeStruct((3 * RAN...  108 us
  transfers between devices with their start and end apart: 1, of which 1 were waited for; matrix products, arithmetic and copies ran while one was open for 1% of the time, Pallas kernels for 0%

profile of v1, /device:TPU:1, one launch (start us, length us, event | category | flops | bytes accessed | tf_op | source)
XLA Modules:
  0.0 284.1 jit_solution(12964217342198200879)
XLA Ops:
  7.2 0.0 all-reduce.3.cloned.1.call-start
  7.2 0.0 copy-start
  7.2 107.5 %attention_gradients.1 = (bf16[192,192]{1,0:T(8,128)(2,1)}, f32[3,64,1536]{2,1,0:T(8,128)}) custom-call(s32[128,128]{1,0:T(8,128)} %mask_ref.1, bf16[192,3072]{1,0:T(8,128)(2,1)} %x_ref.1, bf16[192,1536]{1,0:T(8,128)(2,1)} %q_ref.1, bf16[192,1536]{1,0:T(8,128)(2,1)} %g_ref.1, bf16[192,1536]{1,0:T(8,128)(2,1)} %k_ref.1, bf16[192,1536]{1,0:T(8,128)(2,1)} %v_ref.1, ...), custom_call_target="tpu_custom_call" | custom-call | flops 12000000000 | bytes 8000000 | tf_op jit(solution)/shard_map/attention_gradients/pallas_call | solution.py:435
  114.8 0.0 copy-done
  114.8 0.0 copy-start.3
  114.8 2.9 %convolution_multiply_fusion = f32[192,3072]{1,0:T(8,128)} fusion(bf16[192,192]{1,0:T(8,128)(2,1)} %get-tuple-element.5, bf16[192,3072]{1,0:T(8,128)(2,1)S(1)} %copy-done), kind=kOutput, calls=%fused_computation | convolution fusion | flops 227082240 | bytes 3612672 | tf_op jit(solution)/shard_map/dot_general | solution.py:34
  117.7 0.0 copy-done.3
  117.7 1.1 broadcast_multiply_fusion
  118.8 0.0 copy-start.1
  118.8 0.0 copy-start.4
  118.8 0.0 all-reduce.3.cloned.1.call-update
  118.8 1.2 copy-done.1
  120.1 0.0 copy-done.4
  120.1 1.5 convolution_convert_fusion
  121.6 151.3 %all-reduce.3.cloned.1.call-done = (f32[3,3072,64]{1,2,0:T(8,128)}, f32[3,64,1536]{2,1,0:T(8,128)}) async-done(((f32[3,3072,64]{1,2,0:T(8,128)}, f32[3,64,1536]{2,1,0:T(8,128)}), (f32[3,3072,64]{1,2,0:T(8,128)}, f32[3,64,1536]{2,1,0:T(8,128)})) %all-reduce.3.cloned.1.call-update) | async-done | bytes 3538960 | tf_op jit(solution)/shard_map/psum | solution.py:482
  272.8 0.0 copy-start.2
  272.8 3.4 %copy.13 = f32[3,3072,64]{1,2,0:T(8,128)} copy(f32[3,3072,64]{1,2,0:T(8,128)} %get-tuple-element.10) | data formatting | bytes 4718592
  276.2 0.0 copy-done.2
  276.2 1.0 copy.14
Async XLA Ops:
  7.2 265.7 %all-reduce.3.cloned.1.call-start = ((), (), s32[]{:S(2)}) async-start(), calls=%async_computation | async-start | bytes 7077888 | tf_op jit(solution)/shard_map/psum | solution.py:482
  7.2 107.6 %copy-start = (bf16[192,3072]{1,0:T(8,128)(2,1)S(1)}, bf16[192,3072]{1,0:T(8,128)(2,1)}, u32[]{:S(2)}) copy-start(bf16[192,3072]{1,0:T(8,128)(2,1)} %x_ref.1) | copy-start | bytes 3538948
  114.8 2.9 %copy-start.3 = (f32[3,64,1536]{2,1,0:T(8,128)S(1)}, f32[3,64,1536]{2,1,0:T(8,128)}, u32[]{:S(2)}) copy-start(f32[3,64,1536]{2,1,0:T(8,128)} %get-tuple-element.6) | copy-start | bytes 3538948
  118.8 1.3 copy-start.1
  118.8 1.3 copy-start.4
  272.8 3.4 %copy-start.2 = (f32[3,64,1536]{2,1,0:T(8,128)S(1)}, f32[3,64,1536]{2,1,0:T(8,128)}, u32[]{:S(2)}) copy-start(f32[3,64,1536]{2,1,0:T(8,128)} %get-tuple-element.11) | copy-start | bytes 3538948
Sparse Core Ops, SparseCore 0:
  118.9 153.8 all-reduce.2

commit v2 on v1

--- a/solution.py
+++ b/solution.py
@@ -24,6 +24,11 @@
 TILES = [(0, 512), (512, 512), (1024, 512), (1536, 512), (2048, 512), (2560, 320)]
 ROOT = 1.0 / math.sqrt(DH)
 MASKED = -1e30
+CHIPS = 64
+NORM = 1.0 / math.sqrt(128 * TOK)
+EARLY = 3840
+LATE = 3072
+PIECE = (16, 256)
 
 
 def nt(a, b):
@@ -62,9 +67,11 @@
 
 def attention_kernel(
     mask_ref, x_ref, q_ref, g_ref, k_ref, v_ref, down_ref, up_ref,
-    back_out, upgrad_out,
+    grad_out, down_out, up_out,
     buf, lowbuf, bias, s_ref, d_ref, acc, back0, lowt0, rsend, rrecv,
+    x2, upart, upart2, backs, backs2, terms, result, result2, early_in, late_in, early_sum, late_sum,
     load_sem, send_sem, recv_sem, lsend, lrecv, rs_send, rs_recv,
+    pair_send, pair_recv, red_send, red_recv, gat_send, gat_recv,
 ):
     me = lax.axis_index("frame")
     i = me // 2
@@ -90,21 +97,12 @@
         return pl.ds(s * TOK, TOK)
 
     barrier = pltpu.get_barrier_semaphore()
-    for d in (yp, ym, xp, xm, zp, zm, pt):
-        pl.semaphore_signal(barrier, inc=1, device_id=(d,), device_id_type=MESH)
-    count = jnp.int32(7)
-    for d in SLOT:
-        count = count + pick(valid(d), 1, 0)
-
-        @pl.when(valid(d))
-        def _(d=d):
-            pl.semaphore_signal(barrier, inc=1, device_id=(me - 2 * d,), device_id_type=MESH)
-
-    count = count + pick(side_ok, 1, 0)
-
-    @pl.when(side_ok)
-    def _():
-        pl.semaphore_signal(barrier, inc=1, device_id=(side,), device_id_type=MESH)
+
+    def greet(n, _):
+        pl.semaphore_signal(barrier, inc=1, device_id=((me + n) % 128,), device_id_type=MESH)
+        return 0
+
+    lax.fori_loop(1, 128, greet, 0)
 
     def load(h, a):
         ref = (k_ref, v_ref)[a]
@@ -350,13 +348,19 @@
             acc[RANK:, t0:t0 + w] += nn(gu, pb)
         out0 = (both[:, 0:DH] * ROOT).astype(jnp.bfloat16)
         klow = both[:, DH:DH + RANK] * ROOT
-        upgrad_out[0, :, cols] = nn(lowt0[...], out0)
+        upart[0:RANK, cols] = (nn(lowt0[...], out0) * NORM).astype(jnp.bfloat16)
         back0[...] += nt(up_ref[0, :, cols], out0)
         lows = jnp.concatenate([klow, vlow[:, RANK:]], axis=1).T.astype(jnp.bfloat16)
-        upgrad_out[1, :, cols] = nn(lows[0:RANK], q)
-        upgrad_out[2, :, cols] = nn(lows[RANK:], g)
-
-    pl.semaphore_wait(barrier, count)
+        upart[RANK:2 * RANK, cols] = (nn(lows[0:RANK], q) * NORM).astype(jnp.bfloat16)
+        upart[2 * RANK:, cols] = (nn(lows[RANK:], g) * NORM).astype(jnp.bfloat16)
+
+    pl.semaphore_wait(barrier, 127)
+
+    def pair_copy(n, src, dst):
+        return pltpu.make_async_remote_copy(
+            src_ref=src, dst_ref=dst, send_sem=pair_send.at[n], recv_sem=pair_recv.at[n],
+            device_id=(pt,), device_id_type=MESH,
+        )
 
     last = 4
     order = [16, -16, 4, -4, 1, -1, "z", "y", 8, -8, 2, -2, 32, -32]
@@ -382,6 +386,7 @@
         def _():
             for s, goes, _, to, _ in direct:
                 guarded(goes, low_copy(s, to).start)
+            pair_copy(0, x_ref, x2).start()
 
         @pl.when(r == last)
         def _():
@@ -407,13 +412,163 @@
     for s, _, goes, _, to in direct:
         rsend[s] = acc[:, s * TOK:(s + 1) * TOK].astype(jnp.bfloat16)
         guarded(goes, back_copy(s, to).start)
+    pair_copy(1, upart, upart2).start()
+    backs[0:RANK, :] = back0[...].astype(jnp.bfloat16)
+    pair_copy(2, backs.at[0:RANK], backs2.at[0:RANK]).start()
+    pair_copy(0, x_ref, x2).wait_recv()
+    pair_copy(1, upart, upart2).wait_recv()
+    pair_copy(2, backs.at[0:RANK], backs2.at[0:RANK]).wait_recv()
+
+    def both_up(p, lo, hi):
+        r = slice(p * RANK, (p + 1) * RANK)
+        return (upart[r, lo:hi].astype(jnp.float32) + upart2[r, lo:hi].astype(jnp.float32)).astype(jnp.bfloat16)
+
+    def both_down(p, start):
+        for t in range(0, WIDTH, 512):
+            part = nn(backs[p * RANK:(p + 1) * RANK, :], x_ref[:, t:t + 512])
+            part = part + nn(backs2[p * RANK:(p + 1) * RANK, :], x2[:, t:t + 512])
+            terms[:, start + t:start + t + 512] = (part * NORM).astype(jnp.bfloat16)
+
+    @pl.when(c == 0)
+    def _():
+        both_down(0, 0)
+        terms[:, 3072:3840] = both_up(0, 0, 768)
+
+    @pl.when(c == 1)
+    def _():
+        terms[:, 0:768] = both_up(0, 768, 1536)
+        terms[:, 768:2304] = both_up(1, 0, 1536)
+        terms[:, 2304:3840] = both_up(2, 0, 1536)
+
+    def early_piece(o):
+        return (o % 16) != 15, o - o // 16
+
+    def late_piece(o):
+        oz, ox, oy = o // 16, (o // 4) % 4, o % 4
+        t = (oy - ox - oz + 8) % 4
+        return t < 3, (oz * 4 + ox) * 3 + t
+
+    def place(ref, start, piece):
+        return ref.at[
+            pl.ds(pl.multiple_of((piece % 4) * 16, 16), 16),
+            pl.ds(pl.multiple_of(start + (piece // 4) * 256, 256), 256),
+        ]
+
+    def reduce_start(j, of, start, landing):
+        def one(n, _):
+            o = (i + n) % CHIPS
+            owns, piece = of(o)
+
+            @pl.when(owns)
+            def _():
+                pltpu.make_async_remote_copy(
+                    src_ref=place(terms, start, piece), dst_ref=landing.at[63 - n],
+                    send_sem=red_send.at[j], recv_sem=red_recv.at[j],
+                    device_id=(2 * o + c,), device_id_type=MESH,
+                ).start()
+
+            return 0
+
+        lax.fori_loop(1, CHIPS, one, 0)
+
+    def reduce_finish(j, of, start, landing, sums):
+        owns, piece = of(i)
+
+        @pl.when(owns)
+        def _():
+            pltpu.make_async_copy(landing, landing, red_recv.at[j]).wait()
+            mine = place(terms, start, piece)[...].astype(jnp.float32)
+
+            def add(n, total):
+                return total + landing[n].astype(jnp.float32)
+
+            sums[...] = lax.fori_loop(0, CHIPS - 1, add, mine).astype(jnp.bfloat16)
+            pltpu.make_async_copy(sums, place(result, start, piece), gat_recv.at[j]).start()
+
+            def one(n, _):
+                o = (i + n) % CHIPS
+                pltpu.make_async_remote_copy(
+                    src_ref=sums, dst_ref=place(result, start, piece),
+                    send_sem=gat_send.at[j], recv_sem=gat_recv.at[j],
+                    device_id=(2 * o + c,), device_id_type=MESH,
+                ).start()
+                return 0
+
+            lax.fori_loop(1, CHIPS, one, 0)
+
+    def gathered(j, start, width):
+        part = result.at[:, start:start + width]
+        pltpu.make_async_copy(part, part, gat_recv.at[j]).wait()
+        pair_copy(4 + j, part, result2.at[:, start:start + width]).start()
+
+    def sent(j, of, landing, pieces):
+        owns, _ = of(i)
+
+        @pl.when(owns)
+        def _():
+            part = landing.at[0:pieces - 1]
+            pltpu.make_async_copy(part, part, red_send.at[j]).wait()
+            pltpu.make_async_copy(landing, landing, gat_send.at[j]).wait()
+
+        @pl.when(jnp.logical_not(owns))
+        def _():
+            part = landing.at[0:pieces]
+            pltpu.make_async_copy(part, part, red_send.at[j]).wait()
+
+    reduce_start(0, early_piece, 0, early_in)
+
     total = acc[:, 0:TOK]
     for s, comes_in, _, _, _ in direct:
         guarded(comes_in, back_copy(s, pt).wait_recv)
         total = total + rrecv[s].astype(jnp.float32)
-    back_out[0:RANK, :] = back0[...].astype(jnp.bfloat16)
-    back_out[RANK:, :] = total.astype(jnp.bfloat16)
-
+    backs[RANK:, :] = total.astype(jnp.bfloat16)
+    pair_copy(3, backs.at[RANK:3 * RANK], backs2.at[RANK:3 * RANK]).start()
+    pair_copy(3, backs.at[RANK:3 * RANK], backs2.at[RANK:3 * RANK]).wait_recv()
+
+    @pl.when(c == 0)
+    def _():
+        both_down(1, EARLY)
+
+    @pl.when(c == 1)
+    def _():
+        both_down(2, EARLY)
+
+    reduce_start(1, late_piece, EARLY, late_in)
+    reduce_finish(0, early_piece, 0, early_in, early_sum)
+    back = backs[...].T
+    for t in range(0, WIDTH, 512):
+        grad_out[:, t:t + 512] = nn(back, down_ref[:, t:t + 512]).astype(jnp.bfloat16)
+    reduce_finish(1, late_piece, EARLY, late_in, late_sum)
+    gathered(0, 0, EARLY)
+    gathered(1, EARLY, LATE)
+    for j, (start, width) in enumerate([(0, EARLY), (EARLY, LATE)]):
+        pair_copy(4 + j, result.at[:, start:start + width], result2.at[:, start:start + width]).wait_recv()
+
+    def finish(a, b):
+        down_out[0:RANK, :] = a[:, 0:3072]
+        down_out[RANK:2 * RANK, :] = a[:, 3840:6912]
+        down_out[2 * RANK:, :] = b[:, 3840:6912]
+        up_out[0:RANK, 0:768] = a[:, 3072:3840]
+        up_out[0:RANK, 768:1536] = b[:, 0:768]
+        up_out[RANK:2 * RANK, :] = b[:, 768:2304]
+        up_out[2 * RANK:, :] = b[:, 2304:3840]
+
+    @pl.when(c == 0)
+    def _():
+        finish(result, result2)
+
+    @pl.when(c == 1)
+    def _():
+        finish(result2, result)
+
+    sent(0, early_piece, early_in, 60)
+    sent(1, late_piece, late_in, 48)
+    pair_copy(0, x_ref, x2).wait_send()
+    pair_copy(1, upart, upart2).wait_send()
+    pair_copy(2, backs.at[0:RANK], backs2.at[0:RANK]).wait_send()
+    pair_copy(3, backs.at[RANK:3 * RANK], backs2.at[RANK:3 * RANK]).wait_send()
+    for j, (start, width) in enumerate([(0, EARLY), (EARLY, LATE)]):
+        pair_copy(4 + j, result.at[:, start:start + width], result2.at[:, start:start + width]).wait_send()
     for s, goes, returns, to, owner in direct:
         guarded(goes, low_copy(s, to).wait_send)
         guarded(returns, back_copy(s, owner).wait_send)
@@ -435,12 +590,13 @@
     return pl.pallas_call(
         attention_kernel,
         out_shape=(
-            jax.ShapeDtypeStruct((3 * RANK, TOK), jnp.bfloat16),
-            jax.ShapeDtypeStruct((3, RANK, FEAT), jnp.float32),
+            jax.ShapeDtypeStruct((TOK, WIDTH), jnp.bfloat16),
+            jax.ShapeDtypeStruct((3 * RANK, WIDTH), jnp.bfloat16),
+            jax.ShapeDtypeStruct((3 * RANK, FEAT), jnp.bfloat16),
         ),
         in_specs=[pl.BlockSpec(memory_space=pltpu.SMEM), vm, vm, vm,
                   pl.BlockSpec(memory_space=pl.ANY), pl.BlockSpec(memory_space=pl.ANY), vm, vm],
-        out_specs=(vm, vm),
+        out_specs=(vm, vm, vm),
         scratch_shapes=[
             pltpu.VMEM((HEADS, 2, (SLOTS + 2) * TOK, DH), jnp.bfloat16),
             pltpu.VMEM((KEYS, DH), jnp.bfloat16),
@@ -452,10 +608,23 @@
             pltpu.VMEM((RANK, TOK), jnp.bfloat16),
             pltpu.VMEM((SLOTS, 2 * RANK, TOK), jnp.bfloat16),
             pltpu.VMEM((SLOTS, 2 * RANK, TOK), jnp.bfloat16),
+            pltpu.VMEM((TOK, WIDTH), jnp.bfloat16),
+            pltpu.VMEM((3 * RANK, FEAT), jnp.bfloat16),
+            pltpu.VMEM((3 * RANK, FEAT), jnp.bfloat16),
+            pltpu.VMEM((3 * RANK, TOK), jnp.bfloat16),
+            pltpu.VMEM((3 * RANK, TOK), jnp.bfloat16),
+            pltpu.VMEM((RANK, EARLY + LATE), jnp.bfloat16),
+            pltpu.VMEM((RANK, EARLY + LATE), jnp.bfloat16),
+            pltpu.VMEM((RANK, EARLY + LATE), jnp.bfloat16),
+            pltpu.VMEM((CHIPS - 1, *PIECE), jnp.bfloat16),
+            pltpu.VMEM((CHIPS - 1, *PIECE), jnp.bfloat16),
+            pltpu.VMEM(PIECE, jnp.bfloat16),
+            pltpu.VMEM(PIECE, jnp.bfloat16),
             dma((HEADS, 2)),
             dma((39, HEADS)),
             dma((SLOTS + 2, HEADS)),
             dma((SLOTS,)), dma((SLOTS,)), dma((SLOTS,)), dma((SLOTS,)),
+            dma((6,)), dma((6,)), dma((2,)), dma((2,)), dma((2,)), dma((2,)),
         ],
         compiler_params=pltpu.CompilerParams(
             collective_id=0, has_side_effects=True, vmem_limit_bytes=56 * 2**20
@@ -469,19 +638,13 @@
     inputs, queries, keys, values, output_gradient, radial_block_mask,
     adapter_down_weight, adapter_up_weight,
 ):
-    axis_size = lax.axis_size("frame")
-    norm = 1.0 / math.sqrt(TOK * axis_size)
     down_t = jnp.swapaxes(adapter_down_weight, 1, 2).reshape(3 * RANK, WIDTH)
-    back, up_terms = attention(
+    input_gradient, down, up = attention(
         radial_block_mask, inputs, queries, output_gradient, keys, values, down_t, adapter_up_weight
     )
-    down_terms = nn(back, inputs) * norm
-    input_gradient = lax.dot_general(
-        back, down_t, (((0,), (0,)), ((), ())), preferred_element_type=jnp.float32
-    )
-    down, up = lax.psum((down_terms, up_terms * norm), "frame")
-    down = jnp.swapaxes(down.reshape(3, RANK, WIDTH), 1, 2)
-    return (input_gradient.astype(jnp.bfloat16), down, up)
+    down = jnp.swapaxes(down.reshape(3, RANK, WIDTH), 1, 2).astype(jnp.float32)
+    up = up.reshape(3, RANK, FEAT).astype(jnp.float32)
+    return (input_gradient, down, up)
 
 
 def solution(mesh):

time: 284 us -> 157 us (0.55)
  waiting for transfers between devices: 151 us -> 0 us
  Pallas kernels: 108 us -> 150 us
  between operations: 14.1 us -> 0.65 us
  matrix products: 4.38 us -> 0 us
  local copies, waits for them, and re-layouts: 5.67 us -> 1.57 us
  other arithmetic: 1.13 us -> 4.14 us
    psum x1 -> x0, waiting for transfers between devices: 151 us -> none  [per_device(): down, up = lax.psum((down_terms, up_terms * norm), 'frame')]
    pallas_call x1, Pallas kernels: 108 us -> 150 us  [attention(): pl.pallas_call(attention_kernel, out_shape=(jax.ShapeDtypeStruct((TOK, WI...]
    dot_general x2 -> x0, matrix products: 4.38 us -> none  [the longest x1 2.87 us: nn(): lax.dot_general(a, b, (((1,), (0,)), ((), ())), preferred_element_type=jn...]
    convert_element_type x0 -> x2, other arithmetic: none -> 4.14 us  [the longest x1 3 us: per_device(): down = jnp.swapaxes(down.reshape(3, RANK, WIDTH), 1, 2).astype(jnp.float32)]
    unnamed x12 -> x5, local copies, waits for them, and re-layouts: 5.67 us -> 1.57 us
  transfers between devices with their start and end apart: 1 -> 0, of which waited for: 1 -> 0; matrix products, arithmetic and copies ran while one was open for 1% -> 0% of each run, Pallas kernels for 0% -> 0%
where the time goes in v2:
time: 157 us; the launch traced here: 156 us
  Pallas kernels  150 us (96%)
  other arithmetic  4.14 us (3%)
  local copies, waits for them, and re-layouts  1.57 us (1%)
    pallas_call x1, Pallas kernels, attention(): pl.pallas_call(attention_kernel, out_shape=(jax.ShapeDtypeStruct((TOK, WI...  150 us

profile of v2, /device:TPU:1, one launch (start us, length us, event | category | flops | bytes accessed | tf_op | source)
XLA Modules:
  0.0 156.5 jit_solution(2556638843845822519)
XLA Ops:
  0.6 150.1 %attention_gradients.1 = (bf16[192,3072]{1,0:T(8,128)(2,1)}, bf16[192,3072]{1,0:T(8,128)(2,1)}, bf16[192,1536]{1,0:T(8,128)(2,1)}) custom-call(s32[128,128]{1,0:T(8,128)} %mask_ref.1, bf16[192,3072]{1,0:T(8,128)(2,1)} %x_ref.1, bf16[192,1536]{1,0:T(8,128)(2,1)} %q_ref.1, bf16[192,1536]{1,0:T(8,128)(2,1)} %g_ref.1, bf16[192,1536]{1,0:T(8,128)(2,1)} %k_ref.1, ...), custom_call_target="tpu_custom_call" | custom-call | flops 12000000000 | bytes 8000000 | tf_op jit(solution)/shard_map/attention_gradients/pallas_call | solution.py:590
  150.8 0.0 copy-start.1
  150.8 3.0 %convert_bitcast_fusion = f32[3,3072,64]{1,2,0:T(8,128)} fusion(bf16[3,64,3072]{2,1,0:T(8,128)(2,1)} %bitcast.9), kind=kLoop, calls=%fused_computation | loop fusion | flops 589824 | bytes 3538944 | tf_op jit(solution)/shard_map/convert_element_type | solution.py:645
  153.8 0.0 copy-done.1
  153.8 0.0 copy-start
  153.8 1.1 convert.4
  154.9 0.6 copy-done
  155.5 1.0 copy.12
Async XLA Ops:
  150.8 3.0 %copy-start.1 = (bf16[192,1536]{1,0:T(8,128)(2,1)S(1)}, bf16[192,1536]{1,0:T(8,128)(2,1)}, u32[]{:S(2)}) copy-start(bf16[192,1536]{1,0:T(8,128)(2,1)} %get-tuple-element.8) | copy-start | bytes 1769476
  153.8 1.7 %copy-start = (bf16[192,3072]{1,0:T(8,128)(2,1)S(1)}, bf16[192,3072]{1,0:T(8,128)(2,1)}, u32[]{:S(2)}) copy-start(bf16[192,3072]{1,0:T(8,128)(2,1)} %get-tuple-element.12) | copy-start | bytes 3538948

commit v3 on v2

--- a/solution.py
+++ b/solution.py
@@ -24,9 +24,11 @@
 TILES = [(0, 512), (512, 512), (1024, 512), (1536, 512), (2048, 512), (2560, 320)]
 ROOT = 1.0 / math.sqrt(DH)
 MASKED = -1e30
+LEAD = 1
 CHIPS = 64
 NORM = 1.0 / math.sqrt(128 * TOK)
 EARLY = 3840
+THIRD = EARLY // 3
 LATE = 3072
 PIECE = (16, 256)
 
@@ -66,12 +68,13 @@
 
 
 def attention_kernel(
-    mask_ref, x_ref, q_ref, g_ref, k_ref, v_ref, down_ref, up_ref,
+    mask_ref, x_hbm, q_hbm, g_hbm, k_ref, v_ref, down_hbm, up_hbm,
     grad_out, down_out, up_out,
+    x_ref, q_ref, g_ref, down_ref, up_ref,
     buf, lowbuf, bias, s_ref, d_ref, acc, back0, lowt0, rsend, rrecv,
-    x2, upart, upart2, backs, backs2, terms, result, result2, early_in, late_in, early_sum, late_sum,
-    load_sem, send_sem, recv_sem, lsend, lrecv, rs_send, rs_recv,
-    pair_send, pair_recv, red_send, red_recv, gat_send, gat_recv,
+    x2, upart, upart2, backs, backs2, terms, result, result2, late_in, late_sum, ring1, ring2, ring3, part1, part2, part3,
+    in_sem, load_sem, send_sem, recv_sem, lsend, lrecv, rs_send, rs_recv,
+    pair_send, pair_recv, red_send, red_recv, gat_send, gat_recv, ring_send, ring_recv,
 ):
     me = lax.axis_index("frame")
     i = me // 2
@@ -96,14 +99,6 @@
     def rows(s):
         return pl.ds(s * TOK, TOK)
 
-    barrier = pltpu.get_barrier_semaphore()
-
-    def greet(n, _):
-        pl.semaphore_signal(barrier, inc=1, device_id=((me + n) % 128,), device_id_type=MESH)
-        return 0
-
-    lax.fori_loop(1, 128, greet, 0)
-
     def load(h, a):
         ref = (k_ref, v_ref)[a]
         return pltpu.make_async_copy(
@@ -114,50 +109,20 @@
         for a in range(2):
             load(h, a).start()
 
-    every = [(d, SLOT[d]) for d in SLOT]
-    for d, s in every:
-        @pl.when(jnp.logical_not(valid(d)))
-        def _(s=s):
-            lowbuf[rows(s), :] = jnp.zeros((TOK, DH), jnp.bfloat16)
-            rrecv[s] = jnp.zeros((2 * RANK, TOK), jnp.bfloat16)
-
-            def zero(h, _):
-                for a in range(2):
-                    buf[h, a, rows(s), :] = jnp.zeros((TOK, DH), jnp.bfloat16)
-                return 0
-
-            lax.fori_loop(0, HEADS, zero, 0)
-
-    @pl.when(jnp.logical_not(side_ok))
-    def _():
-        lowbuf[rows(SIDE), :] = jnp.zeros((TOK, DH), jnp.bfloat16)
-        rrecv[SIDE] = jnp.zeros((2 * RANK, TOK), jnp.bfloat16)
-
-        def zero(h, _):
-            for a in range(2):
-                buf[h, a, rows(SIDE), :] = jnp.zeros((TOK, DH), jnp.bfloat16)
-            return 0
-
-        lax.fori_loop(0, HEADS, zero, 0)
-
-    lane = lax.broadcasted_iota(jnp.int32, (8, PAD), 1)
-    total_bias = jnp.zeros((8, PAD), jnp.float32)
-    for s, (block, ok) in enumerate(
-        [(me, None), (pt, None), (side, side_ok)] + [(me - 2 * d, valid(d)) for d in SLOT]
-    ):
-        kept = mask_ref[me, jnp.clip(block, 0, 127)]
-        value = jnp.where(kept > 0, 0.0, MASKED)
-        if ok is not None:
-            value = jnp.where(ok, value, MASKED)
-        inside = (lane >= s * TOK) & (lane < (s + 1) * TOK)
-        total_bias = jnp.where(inside, value, total_bias)
-    bias[...] = total_bias
-
-    low = nt(x_ref[...], down_ref[...]).astype(jnp.bfloat16)
-    lowt0[...] = nt(down_ref[0:RANK, :], x_ref[...]).astype(jnp.bfloat16)
-    lowbuf[rows(OWN), :] = low[:, RANK:]
-    acc[...] = jnp.zeros_like(acc)
-    back0[...] = jnp.zeros_like(back0)
+    def arrays():
+        pairs = [(x_hbm, x_ref), (down_hbm, down_ref), (q_hbm, q_ref), (g_hbm, g_ref), (up_hbm, up_ref)]
+        return [pltpu.make_async_copy(src, dst, in_sem.at[n]) for n, (src, dst) in enumerate(pairs)]
+
+    for one in arrays():
+        one.start()
+
+    barrier = pltpu.get_barrier_semaphore()
+
+    def greet(n, _):
+        pl.semaphore_signal(barrier, inc=1, device_id=((me + n) % 128,), device_id_type=MESH)
+        return 0
+
+    lax.fori_loop(1, 128, greet, 0)
 
     def low_copy(s, device):
         return pltpu.make_async_remote_copy(
@@ -356,6 +321,61 @@
 
     pl.semaphore_wait(barrier, 127)
 
+    def send_own(h):
+        for a in range(2):
+            load(h, a).wait()
+        for k in own:
+            send(k, h)
+
+    lax.fori_loop(0, LEAD, lambda h, _: (send_own(h), 0)[1], 0)
+    for one in arrays():
+        one.wait()
+
+    every = [(d, SLOT[d]) for d in SLOT]
+    for d, s in every:
+        @pl.when(jnp.logical_not(valid(d)))
+        def _(s=s):
+            lowbuf[rows(s), :] = jnp.zeros((TOK, DH), jnp.bfloat16)
+            rrecv[s] = jnp.zeros((2 * RANK, TOK), jnp.bfloat16)
+
+            def zero(h, _):
+                for a in range(2):
+                    buf[h, a, rows(s), :] = jnp.zeros((TOK, DH), jnp.bfloat16)
+                return 0
+
+            lax.fori_loop(0, HEADS, zero, 0)
+
+    @pl.when(jnp.logical_not(side_ok))
+    def _():
+        lowbuf[rows(SIDE), :] = jnp.zeros((TOK, DH), jnp.bfloat16)
+        rrecv[SIDE] = jnp.zeros((2 * RANK, TOK), jnp.bfloat16)
+
+        def zero(h, _):
+            for a in range(2):
+                buf[h, a, rows(SIDE), :] = jnp.zeros((TOK, DH), jnp.bfloat16)
+            return 0
+
+        lax.fori_loop(0, HEADS, zero, 0)
+
+    lane = lax.broadcasted_iota(jnp.int32, (8, PAD), 1)
+    total_bias = jnp.zeros((8, PAD), jnp.float32)
+    for s, (block, ok) in enumerate(
+        [(me, None), (pt, None), (side, side_ok)] + [(me - 2 * d, valid(d)) for d in SLOT]
+    ):
+        kept = mask_ref[me, jnp.clip(block, 0, 127)]
+        value = jnp.where(kept > 0, 0.0, MASKED)
+        if ok is not None:
+            value = jnp.where(ok, value, MASKED)
+        inside = (lane >= s * TOK) & (lane < (s + 1) * TOK)
+        total_bias = jnp.where(inside, value, total_bias)
+    bias[...] = total_bias
+
+    low = nt(x_ref[...], down_ref[...]).astype(jnp.bfloat16)
+    lowt0[...] = nt(down_ref[0:RANK, :], x_ref[...]).astype(jnp.bfloat16)
+    lowbuf[rows(OWN), :] = low[:, RANK:]
+    acc[...] = jnp.zeros_like(acc)
+    back0[...] = jnp.zeros_like(back0)
+
     def pair_copy(n, src, dst):
         return pltpu.make_async_remote_copy(
             src_ref=src, dst_ref=dst, send_sem=pair_send.at[n], recv_sem=pair_recv.at[n],
@@ -366,12 +386,9 @@
     order = [16, -16, 4, -4, 1, -1, "z", "y", 8, -8, 2, -2, 32, -32]
 
     def step(r, _):
-        @pl.when(r < HEADS)
+        @pl.when(r + LEAD < HEADS)
         def _():
-            for a in range(2):
-                load(r, a).wait()
-            for k in own:
-                send(k, r)
+            send_own(r + LEAD)
 
         for d in order:
             h = r - lag(d)
@@ -440,8 +457,65 @@
         terms[:, 768:2304] = both_up(1, 0, 1536)
         terms[:, 2304:3840] = both_up(2, 0, 1536)
 
-    def early_piece(o):
-        return (o % 16) != 15, o - o // 16
+    here = (x, y, z)
+
+    def peer(axis, at):
+        return dev(*(z, at, y, c) if axis == 0 else (z, x, at, c) if axis == 1 else (at, x, y, c))
+
+    def third(ref, k):
+        return ref.at[:, k * THIRD:(k + 1) * THIRD]
+
+    def rows16(ref, n):
+        return ref.at[pl.ds(pl.multiple_of(n * 16, 16), 16), :]
+
+    def ring_copies(stage, k):
+        axis = (k + (0, 1, 2, 0)[stage]) % 3
+        mine = here[axis]
+        out = []
+        for n in (1, 2, 3):
+            to, source = (mine + n) % 4, (mine - n + 4) % 4
+            if stage == 0:
+                src, dst, got = rows16(third(terms, k), to), ring1.at[k, mine], ring1.at[k, source]
+            elif stage == 3:
+                src = part3.at[k]
+                dst, got = rows16(third(result, k), mine), rows16(third(result, k), source)
+            else:
+                ring, part = ((ring2, part1), (ring3, part2))[stage - 1]
+                src, dst, got = part.at[k], ring.at[k, mine], ring.at[k, source]
+            slot = (stage * 3 + k) * 3 + n - 1
+            out.append(tuple(
+                pltpu.make_async_remote_copy(
+                    src_ref=src, dst_ref=where, send_sem=ring_send.at[slot], recv_sem=ring_recv.at[slot],
+                    device_id=(peer(axis, to),), device_id_type=MESH,
+                )
+                for where in (dst, got)
+            ))
+        return out
+
+    def ring_start(stage):
+        for k in range(3):
+            mine = here[(k + (0, 1, 2, 0)[stage]) % 3]
+            if stage == 0:
+                ring1[k, mine] = rows16(third(terms, k), mine)[...]
+            elif stage == 1:
+                ring2[k, mine] = part1[k]
+            elif stage == 2:
+                ring3[k, mine] = part2[k]
+            else:
+                rows16(third(result, k), mine)[...] = part3[k]
+            for out, _ in ring_copies(stage, k):
+                out.start()
+
+    def ring_finish(stage):
+        for k in range(3):
+            for _, got in ring_copies(stage, k):
+                got.wait_recv()
+            if stage < 3:
+                ring, part = ((ring1, part1), (ring2, part2), (ring3, part3))[stage]
+                total = ring[k, 0].astype(jnp.float32)
+                for n in range(1, 4):
+                    total = total + ring[k, n].astype(jnp.float32)
+                part[k] = total.astype(jnp.bfloat16)
 
     def late_piece(o):
         oz, ox, oy = o // 16, (o // 4) % 4, o % 4
@@ -515,7 +589,18 @@
             part = landing.at[0:pieces]
             pltpu.make_async_copy(part, part, red_send.at[j]).wait()
 
-    reduce_start(0, early_piece, 0, early_in)
+    ring_start(0)
+    def drain(h, _):
+        for k, (cond, src, dst, device) in enumerate(kinds):
+            guarded(
+                None if cond is None else cond(h),
+                lambda: copy(k, h, src, dst, device).wait_send(),
+            )
+        return 0
+
+    lax.fori_loop(0, HEADS, drain, 0)
+    ring_finish(0)
+    ring_start(1)
 
     total = acc[:, 0:TOK]
     for s, comes_in, _, _, _ in direct:
@@ -534,12 +619,16 @@
         both_down(2, EARLY)
 
     reduce_start(1, late_piece, EARLY, late_in)
-    reduce_finish(0, early_piece, 0, early_in, early_sum)
+    ring_finish(1)
+    ring_start(2)
     back = backs[...].T
     for t in range(0, WIDTH, 512):
         grad_out[:, t:t + 512] = nn(back, down_ref[:, t:t + 512]).astype(jnp.bfloat16)
+    ring_finish(2)
+    ring_start(3)
     reduce_finish(1, late_piece, EARLY, late_in, late_sum)
-    gathered(0, 0, EARLY)
+    ring_finish(3)
+    pair_copy(4, result.at[:, 0:EARLY], result2.at[:, 0:EARLY]).start()
     gathered(1, EARLY, LATE)
     for j, (start, width) in enumerate([(0, EARLY), (EARLY, LATE)]):
         pair_copy(4 + j, result.at[:, start:start + width], result2.at[:, start:start + width]).wait_recv()
@@ -561,7 +650,10 @@
     def _():
         finish(result2, result)
 
-    sent(0, early_piece, early_in, 60)
+    for stage in range(4):
+        for k in range(3):
+            for out, _ in ring_copies(stage, k):
+                out.wait_send()
     sent(1, late_piece, late_in, 48)
     pair_copy(0, x_ref, x2).wait_send()
     pair_copy(1, upart, upart2).wait_send()
@@ -573,16 +665,6 @@
         guarded(goes, low_copy(s, to).wait_send)
         guarded(returns, back_copy(s, owner).wait_send)
 
-    def drain(h, _):
-        for k, (cond, src, dst, device) in enumerate(kinds):
-            guarded(
-                None if cond is None else cond(h),
-                lambda: copy(k, h, src, dst, device).wait_send(),
-            )
-        return 0
-
-    lax.fori_loop(0, HEADS, drain, 0)
-
 
 def attention(mask, inputs, queries, output_gradient, keys, values, down_t, up):
     vm = pl.BlockSpec(memory_space=pltpu.VMEM)
@@ -594,10 +676,14 @@
             jax.ShapeDtypeStruct((3 * RANK, WIDTH), jnp.bfloat16),
             jax.ShapeDtypeStruct((3 * RANK, FEAT), jnp.bfloat16),
         ),
-        in_specs=[pl.BlockSpec(memory_space=pltpu.SMEM), vm, vm, vm,
-                  pl.BlockSpec(memory_space=pl.ANY), pl.BlockSpec(memory_space=pl.ANY), vm, vm],
+        in_specs=[pl.BlockSpec(memory_space=pltpu.SMEM)] + [pl.BlockSpec(memory_space=pl.ANY)] * 7,
         out_specs=(vm, vm, vm),
         scratch_shapes=[
+            pltpu.VMEM((TOK, WIDTH), jnp.bfloat16),
+            pltpu.VMEM((TOK, FEAT), jnp.bfloat16),
+            pltpu.VMEM((TOK, FEAT), jnp.bfloat16),
+            pltpu.VMEM((3 * RANK, WIDTH), jnp.bfloat16),
+            pltpu.VMEM((3, RANK, FEAT), jnp.bfloat16),
             pltpu.VMEM((HEADS, 2, (SLOTS + 2) * TOK, DH), jnp.bfloat16),
             pltpu.VMEM((KEYS, DH), jnp.bfloat16),
             pltpu.VMEM((8, PAD), jnp.float32),
@@ -617,14 +703,19 @@
             pltpu.VMEM((RANK, EARLY + LATE), jnp.bfloat16),
             pltpu.VMEM((RANK, EARLY + LATE), jnp.bfloat16),
             pltpu.VMEM((CHIPS - 1, *PIECE), jnp.bfloat16),
-            pltpu.VMEM((CHIPS - 1, *PIECE), jnp.bfloat16),
             pltpu.VMEM(PIECE, jnp.bfloat16),
-            pltpu.VMEM(PIECE, jnp.bfloat16),
+            pltpu.VMEM((3, 4, 16, THIRD), jnp.bfloat16),
+            pltpu.VMEM((3, 4, 16, THIRD), jnp.bfloat16),
+            pltpu.VMEM((3, 4, 16, THIRD), jnp.bfloat16),
+            pltpu.VMEM((3, 16, THIRD), jnp.bfloat16),
+            pltpu.VMEM((3, 16, THIRD), jnp.bfloat16),
+            pltpu.VMEM((3, 16, THIRD), jnp.bfloat16),
+            dma((5,)),
             dma((HEADS, 2)),
             dma((39, HEADS)),
             dma((SLOTS + 2, HEADS)),
             dma((SLOTS,)), dma((SLOTS,)), dma((SLOTS,)), dma((SLOTS,)),
-            dma((6,)), dma((6,)), dma((2,)), dma((2,)), dma((2,)), dma((2,)),
+            dma((6,)), dma((6,)), dma((2,)), dma((2,)), dma((2,)), dma((2,)), dma((36,)), dma((36,)),
         ],
         compiler_params=pltpu.CompilerParams(
             collective_id=0, has_side_effects=True, vmem_limit_bytes=56 * 2**20

time: 157 us -> 145 us (0.924)
  Pallas kernels: 150 us -> 138 us
    pallas_call x1, Pallas kernels: 150 us -> 138 us  [attention(): pl.pallas_call(attention_kernel, out_shape=(jax.ShapeDtypeStruct((TOK, WI...]
where the time goes in v3:
time: 145 us
  Pallas kernels  138 us (95%)
  other arithmetic  4.14 us (3%)
  local copies, waits for them, and re-layouts  1.57 us (1%)
    pallas_call x1, Pallas kernels, attention(): pl.pallas_call(attention_kernel, out_shape=(jax.ShapeDtypeStruct((TOK, WI...  138 us
    convert_element_type x1, other arithmetic, per_device(): down = jnp.swapaxes(down.reshape(3, RANK, WIDTH), 1, 2).astype(jnp.float32)  3 us

profile of v3, /device:TPU:1, one launch (start us, length us, event | category | flops | bytes accessed | tf_op | source)
XLA Modules:
  0.0 144.8 jit_solution(7871763427760170473)
XLA Ops:
  0.6 138.4 %attention_gradients.1 = (bf16[192,3072]{1,0:T(8,128)(2,1)}, bf16[192,3072]{1,0:T(8,128)(2,1)}, bf16[192,1536]{1,0:T(8,128)(2,1)}) custom-call(s32[128,128]{1,0:T(8,128)} %mask_ref.1, bf16[192,3072]{1,0:T(8,128)(2,1)} %x_hbm.1, bf16[192,1536]{1,0:T(8,128)(2,1)} %q_hbm.1, bf16[192,1536]{1,0:T(8,128)(2,1)} %g_hbm.1, bf16[192,1536]{1,0:T(8,128)(2,1)} %k_ref.1, ...), custom_call_target="tpu_custom_call" | custom-call | flops 12000000000 | bytes 8000000 | tf_op jit(solution)/shard_map/attention_gradients/pallas_call | solution.py:672
  139.0 0.0 copy-start.1
  139.1 3.0 %convert_bitcast_fusion = f32[3,3072,64]{1,2,0:T(8,128)} fusion(bf16[3,64,3072]{2,1,0:T(8,128)(2,1)} %bitcast.9), kind=kLoop, calls=%fused_computation | loop fusion | flops 589824 | bytes 3538944 | tf_op jit(solution)/shard_map/convert_element_type | solution.py:736
  142.1 0.0 copy-done.1
  142.1 0.0 copy-start
  142.1 1.1 convert.4
  143.2 0.6 copy-done
  143.8 1.0 copy.12
Async XLA Ops:
  139.0 3.0 %copy-start.1 = (bf16[192,1536]{1,0:T(8,128)(2,1)S(1)}, bf16[192,1536]{1,0:T(8,128)(2,1)}, u32[]{:S(2)}) copy-start(bf16[192,1536]{1,0:T(8,128)(2,1)} %get-tuple-element.8) | copy-start | bytes 1769476
  142.1 1.7 %copy-start = (bf16[192,3072]{1,0:T(8,128)(2,1)S(1)}, bf16[192,3072]{1,0:T(8,128)(2,1)}, u32[]{:S(2)}) copy-start(bf16[192,3072]{1,0:T(8,128)(2,1)} %get-tuple-element.12) | copy-start | bytes 3538948

commit v4 on v3

--- a/solution.py
+++ b/solution.py
@@ -25,6 +25,7 @@
 ROOT = 1.0 / math.sqrt(DH)
 MASKED = -1e30
 LEAD = 1
+ITEMS = HEADS + 1
 CHIPS = 64
 NORM = 1.0 / math.sqrt(128 * TOK)
 EARLY = 3840
@@ -68,12 +69,12 @@
 
 
 def attention_kernel(
-    mask_ref, x_hbm, q_hbm, g_hbm, k_ref, v_ref, down_hbm, up_hbm,
+    mask_hbm, x_hbm, q_hbm, g_hbm, k_ref, v_ref, down_hbm, up_hbm,
     grad_out, down_out, up_out,
-    x_ref, q_ref, g_ref, down_ref, up_ref,
+    mask_ref, x_ref, q_ref, g_ref, down_ref, up_ref,
     buf, lowbuf, bias, s_ref, d_ref, acc, back0, lowt0, rsend, rrecv,
     x2, upart, upart2, backs, backs2, terms, result, result2, late_in, late_sum, ring1, ring2, ring3, part1, part2, part3,
-    in_sem, load_sem, send_sem, recv_sem, lsend, lrecv, rs_send, rs_recv,
+    in_sem, load_sem, send_sem, recv_sem, rs_send, rs_recv,
     pair_send, pair_recv, red_send, red_recv, gat_send, gat_recv, ring_send, ring_recv,
 ):
     me = lax.axis_index("frame")
@@ -111,6 +112,7 @@
 
     def arrays():
         pairs = [(x_hbm, x_ref), (down_hbm, down_ref), (q_hbm, q_ref), (g_hbm, g_ref), (up_hbm, up_ref)]
+        pairs += [(mask_hbm.at[pl.ds(me, 1), :], mask_ref)]
         return [pltpu.make_async_copy(src, dst, in_sem.at[n]) for n, (src, dst) in enumerate(pairs)]
 
     for one in arrays():
@@ -123,13 +125,6 @@
         return 0
 
     lax.fori_loop(1, 128, greet, 0)
-
-    def low_copy(s, device):
-        return pltpu.make_async_remote_copy(
-            src_ref=lowbuf.at[rows(OWN)], dst_ref=lowbuf.at[rows(s)],
-            send_sem=lsend.at[s], recv_sem=lrecv.at[s],
-            device_id=(device,), device_id_type=MESH,
-        )
 
     def back_copy(s, device):
         return pltpu.make_async_remote_copy(
@@ -147,12 +142,22 @@
         else:
             pl.when(cond)(f)
 
-    def copy(kind, h, src, dst, device):
-        return pltpu.make_async_remote_copy(
-            src_ref=buf.at[h, :, rows(src)], dst_ref=buf.at[h, :, rows(dst)],
-            send_sem=send_sem.at[kind, h], recv_sem=recv_sem.at[dst, h],
-            device_id=(device,), device_id_type=MESH,
-        )
+    def copy(act, kind, n, src, dst, device):
+        def one(source, target):
+            act(pltpu.make_async_remote_copy(
+                src_ref=source, dst_ref=target,
+                send_sem=send_sem.at[kind, n], recv_sem=recv_sem.at[dst, n],
+                device_id=(device,), device_id_type=MESH,
+            ))
+
+        @pl.when(n == 1)
+        def _():
+            one(lowbuf.at[rows(src)], lowbuf.at[rows(dst)])
+
+        @pl.when(n != 1)
+        def _():
+            h = jnp.maximum(n - 1, 0)
+            one(buf.at[h, :, rows(src)], buf.at[h, :, rows(dst)])
 
     kinds = []
 
@@ -168,8 +173,11 @@
     def by_ring_down(xx, h):
         return (xx == 3) | (((xx == 1) | (xx == 2)) & (h % 2 == 1))
 
-    def late(h):
-        return (h // 2) % 2 == 0
+    def across_up(xx, h):
+        return (xx == 3) | ((h // 2) % 2 == 0)
+
+    def across_down(xx, h):
+        return (xx == 0) | ((h // 2) % 2 == 0)
 
     def up_here(h):
         return by_ring_up(x, h)
@@ -220,7 +228,7 @@
         kind(lambda h: (y == 3) & jnp.logical_not(up_here(h)), SLOT[1], SLOT[-2], yp),
         kind(always((c == 1) & valid(1)), SLOT[1], SIDE, pt),
         kind(
-            lambda h: (y == 3) & (x < 3) & jnp.logical_not(by_ring_up(x + 1, h)) & jnp.logical_not(late(h)),
+            lambda h: (y == 3) & (x < 3) & jnp.logical_not(by_ring_up(x + 1, h)) & jnp.logical_not(across_up(x + 1, h)),
             SLOT[1], VIA_Y, xp,
         ),
     ]
@@ -229,14 +237,14 @@
         kind(lambda h: (y == 0) & up_here(h), SLOT[-1], SLOT[2], ym),
         kind(always((c == 0) & valid(-1)), SLOT[-1], SIDE, pt),
         kind(
-            lambda h: (y == 0) & (x > 0) & jnp.logical_not(by_ring_down(x - 1, h)) & jnp.logical_not(late(h)),
+            lambda h: (y == 0) & (x > 0) & jnp.logical_not(by_ring_down(x - 1, h)) & jnp.logical_not(across_down(x - 1, h)),
             SLOT[-1], VIA_Y, xm,
         ),
     ]
 
     def has_via_y(h):
-        up = (y == 3) & ((z > 0) | (x > 0)) & (up_here(h) | jnp.logical_not(late(h)))
-        down = (y == 0) & ((z < 3) | (x < 3)) & (down_here(h) | jnp.logical_not(late(h)))
+        up = (y == 3) & ((z > 0) | (x > 0)) & (up_here(h) | jnp.logical_not(across_up(x, h)))
+        down = (y == 0) & ((z < 3) | (x < 3)) & (down_here(h) | jnp.logical_not(across_down(x, h)))
         return up | down
 
     via_z = ((z == 3) & (x == 0)) | ((z == 0) & (x == 3))
@@ -245,10 +253,10 @@
         kind(lambda h: (y == 0) & has_via_y(h), VIA_Y, SLOT[-2], ym),
     ]
     on[2] = [
-        kind(lambda h: (y == 3) & (x > 0) & jnp.logical_not(by_ring_down(x - 1, h)) & late(h), SLOT[2], SLOT[-2], xm),
+        kind(lambda h: (y == 3) & (x > 0) & jnp.logical_not(by_ring_down(x - 1, h)) & across_down(x - 1, h), SLOT[2], SLOT[-2], xm),
     ]
     on[-2] = [
-        kind(lambda h: (y == 0) & (x < 3) & jnp.logical_not(by_ring_up(x + 1, h)) & late(h), SLOT[-2], SLOT[2], xp),
+        kind(lambda h: (y == 0) & (x < 3) & jnp.logical_not(by_ring_up(x + 1, h)) & across_up(x + 1, h), SLOT[-2], SLOT[2], xp),
     ]
     on[8] = [kind(always((x == 3) & (z > 0)), SLOT[8], SLOT[-8], zm)]
     on[-8] = [kind(always((x == 0) & (z < 3)), SLOT[-8], SLOT[8], zp)]
@@ -270,10 +278,13 @@
 
     def send(k, h):
         cond, src, dst, device = kinds[k]
-        guarded(None if cond is None else cond(h), lambda: copy(k, h, src, dst, device).start())
+        guarded(
+            None if cond is None else cond(h),
+            lambda: copy(lambda one: one.start(), k, h, src, dst, device),
+        )
 
     def arrived(s, h):
-        copy(0, h, s, s, pt).wait_recv()
+        copy(lambda one: one.wait_recv(), 0, h, s, s, pt)
 
     def head(h):
         cols = pl.ds(pl.multiple_of(h * DH, DH), DH)
@@ -322,13 +333,22 @@
     pl.semaphore_wait(barrier, 127)
 
     def send_own(h):
-        for a in range(2):
-            load(h, a).wait()
+        @pl.when(h != 1)
+        def _():
+            for a in range(2):
+                load(jnp.maximum(h - 1, 0), a).wait()
+
         for k in own:
             send(k, h)
 
-    lax.fori_loop(0, LEAD, lambda h, _: (send_own(h), 0)[1], 0)
-    for one in arrays():
+    send_own(jnp.int32(0))
+    for one in arrays()[:2]:
+        one.wait()
+
+    low = nt(x_ref[...], down_ref[...]).astype(jnp.bfloat16)
+    lowt0[...] = nt(down_ref[0:RANK, :], x_ref[...]).astype(jnp.bfloat16)
+    lowbuf[rows(OWN), :] = low[:, RANK:]
+    for one in arrays()[2:]:
         one.wait()
 
     every = [(d, SLOT[d]) for d in SLOT]
@@ -336,7 +356,7 @@
         @pl.when(jnp.logical_not(valid(d)))
         def _(s=s):
             lowbuf[rows(s), :] = jnp.zeros((TOK, DH), jnp.bfloat16)
-            rrecv[s] = jnp.zeros((2 * RANK, TOK), jnp.bfloat16)
+            rrecv[s] = jnp.zeros((TOK, DH), jnp.bfloat16)
 
             def zero(h, _):
                 for a in range(2):
@@ -348,7 +368,7 @@
     @pl.when(jnp.logical_not(side_ok))
     def _():
         lowbuf[rows(SIDE), :] = jnp.zeros((TOK, DH), jnp.bfloat16)
-        rrecv[SIDE] = jnp.zeros((2 * RANK, TOK), jnp.bfloat16)
+        rrecv[SIDE] = jnp.zeros((TOK, DH), jnp.bfloat16)
 
         def zero(h, _):
             for a in range(2):
@@ -362,7 +382,7 @@
     for s, (block, ok) in enumerate(
         [(me, None), (pt, None), (side, side_ok)] + [(me - 2 * d, valid(d)) for d in SLOT]
     ):
-        kept = mask_ref[me, jnp.clip(block, 0, 127)]
+        kept = mask_ref[0, jnp.clip(block, 0, 127)]
         value = jnp.where(kept > 0, 0.0, MASKED)
         if ok is not None:
             value = jnp.where(ok, value, MASKED)
@@ -370,9 +390,6 @@
         total_bias = jnp.where(inside, value, total_bias)
     bias[...] = total_bias
 
-    low = nt(x_ref[...], down_ref[...]).astype(jnp.bfloat16)
-    lowt0[...] = nt(down_ref[0:RANK, :], x_ref[...]).astype(jnp.bfloat16)
-    lowbuf[rows(OWN), :] = low[:, RANK:]
     acc[...] = jnp.zeros_like(acc)
     back0[...] = jnp.zeros_like(back0)
 
@@ -385,34 +402,36 @@
     last = 4
     order = [16, -16, 4, -4, 1, -1, "z", "y", 8, -8, 2, -2, 32, -32]
 
-    def step(r, _):
-        @pl.when(r + LEAD < HEADS)
-        def _():
-            send_own(r + LEAD)
-
-        for d in order:
+    def handle(slots, r):
+        for d in slots:
             h = r - lag(d)
 
-            @pl.when((h >= 0) & (h < HEADS) & comes(d, h))
+            @pl.when((h >= 0) & (h < ITEMS) & comes(d, h))
             def _(d=d, h=h):
                 arrived(slot_of(d), h)
                 for k in on[d]:
                     send(k, h)
 
+    def step(r, _):
+        @pl.when(r + LEAD < ITEMS)
+        def _():
+            send_own(r + LEAD)
+
+        handle(order[:6], r)
+
+        @pl.when((r >= last + 2) & (r <= HEADS + last + 1))
+        def _():
+            head(r - last - 2)
+
+        handle(order[6:], r)
+
         @pl.when(r == 0)
         def _():
-            for s, goes, _, to, _ in direct:
-                guarded(goes, low_copy(s, to).start)
             pair_copy(0, x_ref, x2).start()
 
-        @pl.when(r == last)
-        def _():
-            for s, _, comes_in, _, _ in direct:
-                guarded(comes_in, low_copy(s, pt).wait_recv)
-
         h = r - last
 
-        @pl.when((h >= 0) & (h < HEADS))
+        @pl.when((h >= 0) & (h < ITEMS))
         def _():
             arrived(PARTNER, h)
 
@@ -420,14 +439,14 @@
             def _():
                 arrived(SIDE, h)
 
-            head(h)
-
         return 0
 
-    lax.fori_loop(0, HEADS + last, step, 0)
+    lax.fori_loop(0, ITEMS + last + 1, step, 0)
 
     for s, _, goes, _, to in direct:
-        rsend[s] = acc[:, s * TOK:(s + 1) * TOK].astype(jnp.bfloat16)
+        part = acc[:, s * TOK:(s + 1) * TOK].astype(jnp.bfloat16)
+        rsend[s, 0:DH, :] = part[:, 0:DH]
+        rsend[s, DH:, :] = jnp.concatenate([part[0:RANK, DH:], part[RANK:, DH:]], axis=1)
         guarded(goes, back_copy(s, to).start)
     pair_copy(1, upart, upart2).start()
     backs[0:RANK, :] = back0[...].astype(jnp.bfloat16)
@@ -594,19 +613,20 @@
         for k, (cond, src, dst, device) in enumerate(kinds):
             guarded(
                 None if cond is None else cond(h),
-                lambda: copy(k, h, src, dst, device).wait_send(),
+                lambda: copy(lambda one: one.wait_send(), k, h, src, dst, device),
             )
         return 0
 
-    lax.fori_loop(0, HEADS, drain, 0)
+    lax.fori_loop(0, ITEMS, drain, 0)
     ring_finish(0)
     ring_start(1)
 
-    total = acc[:, 0:TOK]
+    total = jnp.zeros((TOK, DH), jnp.float32)
     for s, comes_in, _, _, _ in direct:
         guarded(comes_in, back_copy(s, pt).wait_recv)
         total = total + rrecv[s].astype(jnp.float32)
-    backs[RANK:, :] = total.astype(jnp.bfloat16)
+    rest = jnp.concatenate([total[DH:, 0:RANK], total[DH:, RANK:]], axis=0)
+    backs[RANK:, :] = (acc[:, 0:TOK] + jnp.concatenate([total[0:DH], rest], axis=1)).astype(jnp.bfloat16)
     pair_copy(3, backs.at[RANK:3 * RANK], backs2.at[RANK:3 * RANK]).start()
     pair_copy(3, backs.at[RANK:3 * RANK], backs2.at[RANK:3 * RANK]).wait_recv()
 
@@ -628,27 +648,38 @@
     ring_start(3)
     reduce_finish(1, late_piece, EARLY, late_in, late_sum)
     ring_finish(3)
-    pair_copy(4, result.at[:, 0:EARLY], result2.at[:, 0:EARLY]).start()
-    gathered(1, EARLY, LATE)
-    for j, (start, width) in enumerate([(0, EARLY), (EARLY, LATE)]):
-        pair_copy(4 + j, result.at[:, start:start + width], result2.at[:, start:start + width]).wait_recv()
-
-    def finish(a, b):
+
+    def early_pair():
+        return pair_copy(4, result.at[:, 0:EARLY], result2.at[:, 0:EARLY])
+
+    early_pair().start()
+    early_pair().wait_recv()
+
+    def finish_early(a, b):
         down_out[0:RANK, :] = a[:, 0:3072]
-        down_out[RANK:2 * RANK, :] = a[:, 3840:6912]
-        down_out[2 * RANK:, :] = b[:, 3840:6912]
         up_out[0:RANK, 0:768] = a[:, 3072:3840]
         up_out[0:RANK, 768:1536] = b[:, 0:768]
         up_out[RANK:2 * RANK, :] = b[:, 768:2304]
         up_out[2 * RANK:, :] = b[:, 2304:3840]
 
-    @pl.when(c == 0)
-    def _():
-        finish(result, result2)
-
-    @pl.when(c == 1)
-    def _():
-        finish(result2, result)
+    def finish_late(a, b):
+        down_out[RANK:2 * RANK, :] = a[:, EARLY:]
+        down_out[2 * RANK:, :] = b[:, EARLY:]
+
+    def finish(f):
+        @pl.when(c == 0)
+        def _():
+            f(result, result2)
+
+        @pl.when(c == 1)
+        def _():
+            f(result2, result)
+
+    finish(finish_early)
+    gathered(1, EARLY, LATE)
+    late_pair = pair_copy(5, result.at[:, EARLY:], result2.at[:, EARLY:])
+    late_pair.wait_recv()
+    finish(finish_late)
 
     for stage in range(4):
         for k in range(3):
@@ -659,10 +690,9 @@
     pair_copy(1, upart, upart2).wait_send()
     pair_copy(2, backs.at[0:RANK], backs2.at[0:RANK]).wait_send()
     pair_copy(3, backs.at[RANK:3 * RANK], backs2.at[RANK:3 * RANK]).wait_send()
-    for j, (start, width) in enumerate([(0, EARLY), (EARLY, LATE)]):
-        pair_copy(4 + j, result.at[:, start:start + width], result2.at[:, start:start + width]).wait_send()
+    early_pair().wait_send()
+    late_pair.wait_send()
     for s, goes, returns, to, owner in direct:
-        guarded(goes, low_copy(s, to).wait_send)
         guarded(returns, back_copy(s, owner).wait_send)
 
 
@@ -676,24 +706,25 @@
             jax.ShapeDtypeStruct((3 * RANK, WIDTH), jnp.bfloat16),
             jax.ShapeDtypeStruct((3 * RANK, FEAT), jnp.bfloat16),
         ),
-        in_specs=[pl.BlockSpec(memory_space=pltpu.SMEM)] + [pl.BlockSpec(memory_space=pl.ANY)] * 7,
+        in_specs=[pl.BlockSpec(memory_space=pl.ANY)] * 8,
         out_specs=(vm, vm, vm),
         scratch_shapes=[
+            pltpu.SMEM((1, 128), jnp.int32),
             pltpu.VMEM((TOK, WIDTH), jnp.bfloat16),
             pltpu.VMEM((TOK, FEAT), jnp.bfloat16),
             pltpu.VMEM((TOK, FEAT), jnp.bfloat16),
             pltpu.VMEM((3 * RANK, WIDTH), jnp.bfloat16),
             pltpu.VMEM((3, RANK, FEAT), jnp.bfloat16),
             pltpu.VMEM((HEADS, 2, (SLOTS + 2) * TOK, DH), jnp.bfloat16),
-            pltpu.VMEM((KEYS, DH), jnp.bfloat16),
+            pltpu.VMEM((KEYS + 2 * TOK, DH), jnp.bfloat16),
             pltpu.VMEM((8, PAD), jnp.float32),
             pltpu.VMEM((TOK, PAD), jnp.float32),
             pltpu.VMEM((TOK, PAD), jnp.float32),
             pltpu.VMEM((2 * RANK, PAD), jnp.float32),
             pltpu.VMEM((RANK, TOK), jnp.float32),
             pltpu.VMEM((RANK, TOK), jnp.bfloat16),
-            pltpu.VMEM((SLOTS, 2 * RANK, TOK), jnp.bfloat16),
-            pltpu.VMEM((SLOTS, 2 * RANK, TOK), jnp.bfloat16),
+            pltpu.VMEM((SLOTS, TOK, DH), jnp.bfloat16),
+            pltpu.VMEM((SLOTS, TOK, DH), jnp.bfloat16),
             pltpu.VMEM((TOK, WIDTH), jnp.bfloat16),
             pltpu.VMEM((3 * RANK, FEAT), jnp.bfloat16),
             pltpu.VMEM((3 * RANK, FEAT), jnp.bfloat16),
@@ -710,11 +741,11 @@
             pltpu.VMEM((3, 16, THIRD), jnp.bfloat16),
             pltpu.VMEM((3, 16, THIRD), jnp.bfloat16),
             pltpu.VMEM((3, 16, THIRD), jnp.bfloat16),
-            dma((5,)),
+            dma((6,)),
             dma((HEADS, 2)),
-            dma((39, HEADS)),
-            dma((SLOTS + 2, HEADS)),
-            dma((SLOTS,)), dma((SLOTS,)), dma((SLOTS,)), dma((SLOTS,)),
+            dma((39, ITEMS)),
+            dma((SLOTS + 2, ITEMS)),
+            dma((SLOTS,)), dma((SLOTS,)),
             dma((6,)), dma((6,)), dma((2,)), dma((2,)), dma((2,)), dma((2,)), dma((36,)), dma((36,)),
         ],
         compiler_params=pltpu.CompilerParams(

time: 145 us -> 137 us (0.945)
  Pallas kernels: 138 us -> 130 us
    pallas_call x1, Pallas kernels: 138 us -> 130 us  [attention(): pl.pallas_call(attention_kernel, out_shape=(jax.ShapeDtypeStruct((TOK, WI...]
where the time goes in v4:
time: 137 us; the launch traced here: 136 us
  Pallas kernels  130 us (95%)
  other arithmetic  4.14 us (3%)
  local copies, waits for them, and re-layouts  1.57 us (1%)
    pallas_call x1, Pallas kernels, attention(): pl.pallas_call(attention_kernel, out_shape=(jax.ShapeDtypeStruct((TOK, WI...  130 us
    convert_element_type x1, other arithmetic, per_device(): down = jnp.swapaxes(down.reshape(3, RANK, WIDTH), 1, 2).astype(jnp.float32)  3 us

profile of v4, /device:TPU:1, one launch (start us, length us, event | category | flops | bytes accessed | tf_op | source)
XLA Modules:
  0.0 136.4 jit_solution(17986175361796075565)
XLA Ops:
  0.6 130.1 %attention_gradients.1 = (bf16[192,3072]{1,0:T(8,128)(2,1)}, bf16[192,3072]{1,0:T(8,128)(2,1)}, bf16[192,1536]{1,0:T(8,128)(2,1)}) custom-call(s32[128,128]{1,0:T(8,128)} %mask_hbm.1, bf16[192,3072]{1,0:T(8,128)(2,1)} %x_hbm.1, bf16[192,1536]{1,0:T(8,128)(2,1)} %q_hbm.1, bf16[192,1536]{1,0:T(8,128)(2,1)} %g_hbm.1, bf16[192,1536]{1,0:T(8,128)(2,1)} %k_ref.1, ...), custom_call_target="tpu_custom_call" | custom-call | flops 12000000000 | bytes 8000000 | tf_op jit(solution)/shard_map/attention_gradients/pallas_call | solution.py:702
  130.7 0.0 copy-start.1
  130.7 3.0 %convert_bitcast_fusion = f32[3,3072,64]{1,2,0:T(8,128)} fusion(bf16[3,64,3072]{2,1,0:T(8,128)(2,1)} %bitcast.9), kind=kLoop, calls=%fused_computation | loop fusion | flops 589824 | bytes 3538944 | tf_op jit(solution)/shard_map/convert_element_type | solution.py:767
  133.7 0.0 copy-done.1
  133.7 0.0 copy-start
  133.7 1.1 convert.4
  134.9 0.6 copy-done
  135.4 1.0 copy.12
Async XLA Ops:
  130.7 3.0 %copy-start.1 = (bf16[192,1536]{1,0:T(8,128)(2,1)S(1)}, bf16[192,1536]{1,0:T(8,128)(2,1)}, u32[]{:S(2)}) copy-start(bf16[192,1536]{1,0:T(8,128)(2,1)} %get-tuple-element.8) | copy-start | bytes 1769476
  133.7 1.7 %copy-start = (bf16[192,3072]{1,0:T(8,128)(2,1)S(1)}, bf16[192,3072]{1,0:T(8,128)(2,1)}, u32[]{:S(2)}) copy-start(bf16[192,3072]{1,0:T(8,128)(2,1)} %get-tuple-element.12) | copy-start | bytes 3538948

commit v5 on v4

--- a/solution.py
+++ b/solution.py
@@ -756,17 +756,43 @@
     )(mask, inputs, queries, output_gradient, keys, values, down_t, up)
 
 
+def finish_kernel(grad_in, down_in, up_in, grad, down, up):
+    grad[...] = grad_in[...]
+    down[...] = down_in[...].astype(jnp.float32)
+    up[...] = up_in[...].astype(jnp.float32)
+
+
+def finished(grad, down, up):
+    parts = 3
+
+    def block(width):
+        return pl.BlockSpec((TOK, width // parts), lambda n: (0, n))
+
+    specs = [block(WIDTH), block(WIDTH), block(FEAT)]
+    return pl.pallas_call(
+        finish_kernel,
+        grid=(parts,),
+        out_shape=(
+            jax.ShapeDtypeStruct(grad.shape, grad.dtype),
+            jax.ShapeDtypeStruct(down.shape, jnp.float32),
+            jax.ShapeDtypeStruct(up.shape, jnp.float32),
+        ),
+        in_specs=specs,
+        out_specs=specs,
+        name="final_types",
+    )(grad, down, up)
+
+
 def per_device(
     inputs, queries, keys, values, output_gradient, radial_block_mask,
     adapter_down_weight, adapter_up_weight,
 ):
     down_t = jnp.swapaxes(adapter_down_weight, 1, 2).reshape(3 * RANK, WIDTH)
-    input_gradient, down, up = attention(
+    input_gradient, down, up = finished(*attention(
         radial_block_mask, inputs, queries, output_gradient, keys, values, down_t, adapter_up_weight
-    )
-    down = jnp.swapaxes(down.reshape(3, RANK, WIDTH), 1, 2).astype(jnp.float32)
-    up = up.reshape(3, RANK, FEAT).astype(jnp.float32)
-    return (input_gradient, down, up)
+    ))
+    down = jnp.swapaxes(down.reshape(3, RANK, WIDTH), 1, 2)
+    return (input_gradient, down, up.reshape(3, RANK, FEAT))
 
 
 def solution(mesh):

time: 137 us -> 135 us (0.985)
  Pallas kernels: 130 us -> 135 us
  other arithmetic: 4.14 us -> 0 us
  local copies, waits for them, and re-layouts: 1.57 us -> 0 us
    pallas_call x0 -> x1, Pallas kernels: none -> 4.49 us  [finished(): pl.pallas_call(finish_kernel, grid=(parts,), out_shape=(jax.ShapeDtypeStr...]
    convert_element_type x2 -> x0, other arithmetic: 4.14 us -> none  [the longest x1 3 us: per_device(): down = jnp.swapaxes(down.reshape(3, RANK, WIDTH), 1, 2).astype(jnp.float32)]
    unnamed x5 -> x0, local copies, waits for them, and re-layouts: 1.57 us -> none
where the time goes in v5:
time: 135 us
  Pallas kernels  135 us (100%)
    pallas_call x1, Pallas kernels, attention(): pl.pallas_call(attention_kernel, out_shape=(jax.ShapeDtypeStruct((TOK, WI...  130 us
    pallas_call x1, Pallas kernels, finished(): pl.pallas_call(finish_kernel, grid=(parts,), out_shape=(jax.ShapeDtypeStr...  4.49 us

profile of v5, /device:TPU:1, one launch (start us, length us, event | category | flops | bytes accessed | tf_op | source)
XLA Modules:
  0.0 135.2 jit_solution(16224795730583781897)
XLA Ops:
  0.6 130.1 %attention_gradients.1 = (bf16[192,3072]{1,0:T(8,128)(2,1)}, bf16[192,3072]{1,0:T(8,128)(2,1)}, bf16[192,1536]{1,0:T(8,128)(2,1)}) custom-call(s32[128,128]{1,0:T(8,128)} %mask_hbm.1, bf16[192,3072]{1,0:T(8,128)(2,1)} %x_hbm.1, bf16[192,1536]{1,0:T(8,128)(2,1)} %q_hbm.1, bf16[192,1536]{1,0:T(8,128)(2,1)} %g_hbm.1, bf16[192,1536]{1,0:T(8,128)(2,1)} %k_ref.1, ...), custom_call_target="tpu_custom_call" | custom-call | flops 12000000000 | bytes 8000000 | tf_op jit(solution)/shard_map/attention_gradients/pallas_call | solution.py:702
  130.7 4.5 %final_types.1 = (bf16[192,3072]{1,0:T(8,128)(2,1)}, f32[192,3072]{1,0:T(8,128)}, f32[192,1536]{1,0:T(8,128)}) custom-call(bf16[192,3072]{1,0:T(8,128)(2,1)} %get-tuple-element.9.grad_in, bf16[192,3072]{1,0:T(8,128)(2,1)} %get-tuple-element.10.down_in, bf16[192,1536]{1,0:T(8,128)(2,1)} %get-tuple-element.11.up_in), custom_call_target="tpu_custom_call" | custom-call | tf_op jit(solution)/shard_map/final_types/pallas_call | solution.py:772

commit v6 on v5

--- a/solution.py
+++ b/solution.py
@@ -70,8 +70,8 @@
 
 def attention_kernel(
     mask_hbm, x_hbm, q_hbm, g_hbm, k_ref, v_ref, down_hbm, up_hbm,
-    grad_out, down_out, up_out,
-    mask_ref, x_ref, q_ref, g_ref, down_ref, up_ref,
+    grad_hbm, down_out, up_out,
+    grad_out, grad_sem, mask_ref, x_ref, q_ref, g_ref, down_ref, up_ref,
     buf, lowbuf, bias, s_ref, d_ref, acc, back0, lowt0, rsend, rrecv,
     x2, upart, upart2, backs, backs2, terms, result, result2, late_in, late_sum, ring1, ring2, ring3, part1, part2, part3,
     in_sem, load_sem, send_sem, recv_sem, rs_send, rs_recv,
@@ -124,7 +124,7 @@
         pl.semaphore_signal(barrier, inc=1, device_id=((me + n) % 128,), device_id_type=MESH)
         return 0
 
-    lax.fori_loop(1, 128, greet, 0)
+    lax.fori_loop(1, 128, greet, 0, unroll=True)
 
     def back_copy(s, device):
         return pltpu.make_async_remote_copy(
@@ -644,6 +644,8 @@
     back = backs[...].T
     for t in range(0, WIDTH, 512):
         grad_out[:, t:t + 512] = nn(back, down_ref[:, t:t + 512]).astype(jnp.bfloat16)
+    leave = pltpu.make_async_copy(grad_out, grad_hbm, grad_sem)
+    leave.start()
     ring_finish(2)
     ring_start(3)
     reduce_finish(1, late_piece, EARLY, late_in, late_sum)
@@ -690,6 +692,7 @@
     pair_copy(1, upart, upart2).wait_send()
     pair_copy(2, backs.at[0:RANK], backs2.at[0:RANK]).wait_send()
     pair_copy(3, backs.at[RANK:3 * RANK], backs2.at[RANK:3 * RANK]).wait_send()
+    leave.wait()
     early_pair().wait_send()
     late_pair.wait_send()
     for s, goes, returns, to, owner in direct:
@@ -707,8 +710,10 @@
             jax.ShapeDtypeStruct((3 * RANK, FEAT), jnp.bfloat16),
         ),
         in_specs=[pl.BlockSpec(memory_space=pl.ANY)] * 8,
-        out_specs=(vm, vm, vm),
+        out_specs=(pl.BlockSpec(memory_space=pl.ANY), vm, vm),
         scratch_shapes=[
+            pltpu.VMEM((TOK, WIDTH), jnp.bfloat16),
+            dma,
             pltpu.SMEM((1, 128), jnp.int32),
             pltpu.VMEM((TOK, WIDTH), jnp.bfloat16),
             pltpu.VMEM((TOK, FEAT), jnp.bfloat16),

time: 135 us -> 135 us (level)
  no operation moved by 1% of the time
where the time goes in v6:
time: 135 us; the launch traced here: 134 us
  Pallas kernels  134 us (99%)
    pallas_call x1, Pallas kernels, attention(): pl.pallas_call(attention_kernel, out_shape=(jax.ShapeDtypeStruct((TOK, WI...  129 us
    pallas_call x1, Pallas kernels, finished(): pl.pallas_call(finish_kernel, grid=(parts,), out_shape=(jax.ShapeDtypeStr...  4.49 us

profile of v6, /device:TPU:1, one launch (start us, length us, event | category | flops | bytes accessed | tf_op | source)
XLA Modules:
  0.0 134.5 jit_solution(12104176882562000817)
XLA Ops:
  0.6 129.3 %attention_gradients.1 = (bf16[192,3072]{1,0:T(8,128)(2,1)}, bf16[192,3072]{1,0:T(8,128)(2,1)}, bf16[192,1536]{1,0:T(8,128)(2,1)}) custom-call(s32[128,128]{1,0:T(8,128)} %mask_hbm.1, bf16[192,3072]{1,0:T(8,128)(2,1)} %x_hbm.1, bf16[192,1536]{1,0:T(8,128)(2,1)} %q_hbm.1, bf16[192,1536]{1,0:T(8,128)(2,1)} %g_hbm.1, bf16[192,1536]{1,0:T(8,128)(2,1)} %k_ref.1, ...), custom_call_target="tpu_custom_call" | custom-call | flops 12000000000 | bytes 8000000 | tf_op jit(solution)/shard_map/attention_gradients/pallas_call | solution.py:705
  130.0 4.5 %final_types.1 = (bf16[192,3072]{1,0:T(8,128)(2,1)}, f32[192,3072]{1,0:T(8,128)}, f32[192,1536]{1,0:T(8,128)}) custom-call(bf16[192,3072]{1,0:T(8,128)(2,1)} %get-tuple-element.9.grad_in, bf16[192,3072]{1,0:T(8,128)(2,1)} %get-tuple-element.10.down_in, bf16[192,1536]{1,0:T(8,128)(2,1)} %get-tuple-element.11.up_in), custom_call_target="tpu_custom_call" | custom-call | tf_op jit(solution)/shard_map/final_types/pallas_call | solution.py:777

commit v7 on v6

--- a/solution.py
+++ b/solution.py
@@ -459,14 +459,18 @@
         r = slice(p * RANK, (p + 1) * RANK)
         return (upart[r, lo:hi].astype(jnp.float32) + upart2[r, lo:hi].astype(jnp.float32)).astype(jnp.bfloat16)
 
+    def own_down(p):
+        for t in range(0, WIDTH, 512):
+            s_ref[0:RANK, t:t + 512] = nn(backs[p * RANK:(p + 1) * RANK, :], x_ref[:, t:t + 512])
+
     def both_down(p, start):
         for t in range(0, WIDTH, 512):
-            part = nn(backs[p * RANK:(p + 1) * RANK, :], x_ref[:, t:t + 512])
-            part = part + nn(backs2[p * RANK:(p + 1) * RANK, :], x2[:, t:t + 512])
+            part = s_ref[0:RANK, t:t + 512] + nn(backs2[p * RANK:(p + 1) * RANK, :], x2[:, t:t + 512])
             terms[:, start + t:start + t + 512] = (part * NORM).astype(jnp.bfloat16)
 
     @pl.when(c == 0)
     def _():
+        own_down(0)
         both_down(0, 0)
         terms[:, 3072:3840] = both_up(0, 0, 768)
 
@@ -575,7 +579,7 @@
             def add(n, total):
                 return total + landing[n].astype(jnp.float32)
 
-            sums[...] = lax.fori_loop(0, CHIPS - 1, add, mine).astype(jnp.bfloat16)
+            sums[...] = lax.fori_loop(0, CHIPS - 1, add, mine, unroll=9).astype(jnp.bfloat16)
             pltpu.make_async_copy(sums, place(result, start, piece), gat_recv.at[j]).start()
 
             def one(n, _):
@@ -628,6 +632,15 @@
     rest = jnp.concatenate([total[DH:, 0:RANK], total[DH:, RANK:]], axis=0)
     backs[RANK:, :] = (acc[:, 0:TOK] + jnp.concatenate([total[0:DH], rest], axis=1)).astype(jnp.bfloat16)
     pair_copy(3, backs.at[RANK:3 * RANK], backs2.at[RANK:3 * RANK]).start()
+
+    @pl.when(c == 0)
+    def _():
+        own_down(1)
+
+    @pl.when(c == 1)
+    def _():
+        own_down(2)
+
     pair_copy(3, backs.at[RANK:3 * RANK], backs2.at[RANK:3 * RANK]).wait_recv()
 
     @pl.when(c == 0)

time: 135 us -> 135 us (level)
  no operation moved by 1% of the time
where the time goes in v7:
time: 135 us; the launch traced here: 134 us
  Pallas kernels  134 us (99%)
    pallas_call x1, Pallas kernels, attention(): pl.pallas_call(attention_kernel, out_shape=(jax.ShapeDtypeStruct((TOK, WI...  129 us
    pallas_call x1, Pallas kernels, finished(): pl.pallas_call(finish_kernel, grid=(parts,), out_shape=(jax.ShapeDtypeStr...  4.49 us

profile of v7, /device:TPU:1, one launch (start us, length us, event | category | flops | bytes accessed | tf_op | source)
XLA Modules:
  0.0 134.3 jit_solution(1071711180469781752)
XLA Ops:
  0.6 129.2 %attention_gradients.1 = (bf16[192,3072]{1,0:T(8,128)(2,1)}, bf16[192,3072]{1,0:T(8,128)(2,1)}, bf16[192,1536]{1,0:T(8,128)(2,1)}) custom-call(s32[128,128]{1,0:T(8,128)} %mask_hbm.1, bf16[192,3072]{1,0:T(8,128)(2,1)} %x_hbm.1, bf16[192,1536]{1,0:T(8,128)(2,1)} %q_hbm.1, bf16[192,1536]{1,0:T(8,128)(2,1)} %g_hbm.1, bf16[192,1536]{1,0:T(8,128)(2,1)} %k_ref.1, ...), custom_call_target="tpu_custom_call" | custom-call | flops 12000000000 | bytes 8000000 | tf_op jit(solution)/shard_map/attention_gradients/pallas_call | solution.py:718
  129.8 4.5 %final_types.1 = (bf16[192,3072]{1,0:T(8,128)(2,1)}, f32[192,3072]{1,0:T(8,128)}, f32[192,1536]{1,0:T(8,128)}) custom-call(bf16[192,3072]{1,0:T(8,128)(2,1)} %get-tuple-element.9.grad_in, bf16[192,3072]{1,0:T(8,128)(2,1)} %get-tuple-element.10.down_in, bf16[192,1536]{1,0:T(8,128)(2,1)} %get-tuple-element.11.up_in), custom_call_target="tpu_custom_call" | custom-call | tf_op jit(solution)/shard_map/final_types/pallas_call | solution.py:790
